TPU v7x, 128 devices: a whole 4x4x4 slice. The times are simulated.
128 devices in a mesh: gx: 4 (over z), gy: 4 (over x), gz: 8 (over y, core).
Axes of the slice: x: 4, y: 4, z: 4, core: 2. Of those that a mesh axis runs over, the one named last changes fastest.
Arguments:
- density_blocks: bfloat16 [4096, 128, 128], P(('gx', 'gy', 'gz')), may hold values from -0.00625 to 0.00625
- orbital_values: bfloat16 [64, 64, 128, 1280], P('gx', 'gy', 'gz'), may hold values from -11 to 11
- pair_index: int32 [128, 100], P(('gx', 'gy', 'gz')), may hold values from 0 to 4095, as said below
Outputs:
- potential_blocks: float32 [4096, 128, 128], P(('gx', 'gy', 'gz'))
- potential: float32 [64, 64, 128], P('gx', 'gy', 'gz')
Inputs may be any that keep to these rules, and one draw needn't show every extreme that they name: `pair_index`: A domain's 100 entries are distinct. Each domain names at most 2 blocks held by one device, and exactly 2 for some holder.
All inputs are finite; a program needn't handle non-finite values.
Results may differ from a plain program's by a relative error of at most 0.0034.
Values may be sent and summed in bfloat16 or wider, within the bound.
A program may use at most 128 MiB of HBM per device.

v0:
```python
import jax
import jax.numpy as jnp
from jax import lax
from jax.sharding import PartitionSpec as P

ORB_BLOCKS = 10
NPRE = 2
NCOARSE = 4
NPOST = 2


OMEGA = 0.6
SCREEN = 0.05


def with_halo(block, sides, width):
    for axis, dim in sides:
        count = lax.axis_size(axis)
        forward = [(i, i + 1) for i in range(count - 1)]
        forward.append((count - 1, 0))
        backward = [(target, source) for source, target in forward]
        low = lax.ppermute(
            lax.slice_in_dim(block, block.shape[dim] - width, None, axis=dim), axis, forward
        )
        high = lax.ppermute(lax.slice_in_dim(block, 0, width, axis=dim), axis, backward)
        block = jnp.concatenate([low, block, high], axis=dim)
    return block


def stencil(padded, center, diag):
    beside = padded[2:, 1:-1, 1:-1] + padded[:-2, 1:-1, 1:-1]
    beside = beside + padded[1:-1, 2:, 1:-1] + padded[1:-1, :-2, 1:-1]
    beside = beside + padded[1:-1, 1:-1, 2:] + padded[1:-1, 1:-1, :-2]
    return diag * center - beside


def fine_image(field, diag):
    padded = with_halo(field, (("gx", 0), ("gy", 1), ("gz", 2)), 1)
    return stencil(padded, field, diag)


def coarse_image(field, diag):
    padded = with_halo(field, (("gx", 0), ("gy", 1), ("gz", 2)), 1)
    return stencil(padded, field, diag)


def deliver(buffer):
    return lax.all_to_all(buffer, ("gx", "gy", "gz"), split_axis=0, concat_axis=0, tiled=True)


def body(density_blocks, orbital_values, pair_index):
    ndev = lax.axis_size(("gx", "gy", "gz"))
    device = lax.axis_index(("gx", "gy", "gz"))
    nnz_dev = density_blocks.shape[0]
    block = density_blocks.shape[1]
    npair = pair_index.shape[1]
    spread = min(ndev, npair // 2)
    cap = (npair + spread - 1) // spread
    requests = lax.all_gather(pair_index, ("gx", "gy", "gz"), axis=0, tiled=True)
    holder = requests // nnz_dev
    held_slot = requests % nnz_dev
    order = jnp.arange(npair, dtype=jnp.int32)
    before = order[None, :] < order[:, None]
    rank = jnp.sum((holder[:, :, None] == holder[:, None, :]) & before[None], axis=2)
    places = jnp.arange(cap, dtype=jnp.int32)
    wanted = (holder[:, None, :] == device) & (rank[:, None, :] == places[None, :, None])
    filled = jnp.any(wanted, axis=2)
    source_slot = jnp.sum(jnp.where(wanted, held_slot[:, None, :], 0), axis=2)
    outgoing = jnp.where(
        filled[:, :, None, None], density_blocks[source_slot], jnp.zeros((), density_blocks.dtype)
    )
    incoming = deliver(outgoing)
    own_holder = lax.dynamic_index_in_dim(holder, device, 0, keepdims=False)
    own_rank = lax.dynamic_index_in_dim(rank, device, 0, keepdims=False)
    position = own_holder * cap + own_rank
    local_blocks = incoming.reshape(ndev * cap, block, block)[position]
    local_matrix = (
        local_blocks.reshape(ORB_BLOCKS, ORB_BLOCKS, block, block)
        .transpose(0, 2, 1, 3)
        .reshape(ORB_BLOCKS * block, ORB_BLOCKS * block)
    )
    size_x, size_y, size_z, local_orb = orbital_values.shape
    cells = size_x * size_y * size_z
    orbitals = orbital_values.reshape(cells, local_orb)
    product = jnp.dot(orbitals, local_matrix, preferred_element_type=jnp.float32)
    density = jnp.sum(orbitals * product, axis=1).reshape(size_x, size_y, size_z)
    total = lax.psum(jnp.sum(density), ("gx", "gy", "gz"))
    source = density - total / (cells * ndev)
    fine_diag = 6.0 + SCREEN
    coarse_diag = 6.0 + 4.0 * SCREEN
    field = jnp.zeros_like(source)
    for sweep_index in range(NPRE):
        field = field + OMEGA * (source - fine_image(field, fine_diag)) / fine_diag
    residual = source - fine_image(field, fine_diag)
    coarse_source = 4.0 * jnp.mean(
        residual.reshape(size_x // 2, 2, size_y // 2, 2, size_z // 2, 2), axis=(1, 3, 5)
    )
    correction = jnp.zeros_like(coarse_source)
    for sweep_index in range(NCOARSE):
        correction = (
            correction
            + OMEGA * (coarse_source - coarse_image(correction, coarse_diag)) / coarse_diag
        )
    field = field + jnp.repeat(jnp.repeat(jnp.repeat(correction, 2, 0), 2, 1), 2, 2)
    for sweep_index in range(NPOST):
        field = field + OMEGA * (source - fine_image(field, fine_diag)) / fine_diag
    weighted = (field.reshape(-1)[:, None] * orbitals).astype(jnp.bfloat16)
    matrix = lax.dot_general(
        orbitals, weighted, (((0,), (0,)), ((), ())), preferred_element_type=jnp.float32
    ) * cells ** (-0.5)
    pieces = (
        matrix.reshape(ORB_BLOCKS, block, ORB_BLOCKS, block)
        .transpose(0, 2, 1, 3)
        .reshape(npair, block, block)
        .astype(jnp.bfloat16)
    )
    returning = jnp.zeros((ndev * cap, block, block), jnp.bfloat16).at[position].set(pieces)
    arrived = deliver(returning.reshape(ndev, cap, block, block))
    slots = jnp.arange(nnz_dev, dtype=jnp.int32)
    selector = (
        filled.reshape(-1)[None, :] & (source_slot.reshape(-1)[None, :] == slots[:, None])
    ).astype(jnp.bfloat16)
    summed = jnp.dot(
        selector, arrived.reshape(ndev * cap, block * block), preferred_element_type=jnp.float32
    )
    return (summed.reshape(nnz_dev, block, block), field)


def solution(mesh):
    return jax.shard_map(
        body,
        mesh=mesh,
        in_specs=(
            P(("gx", "gy", "gz"), None, None),
            P("gx", "gy", "gz", None),
            P(("gx", "gy", "gz"), None),
        ),
        out_specs=(P(("gx", "gy", "gz"), None, None), P("gx", "gy", "gz")),
        check_vma=False,
    )
```

profile of v0, /device:TPU:0, one launch (start us, length us, event | category | flops | bytes accessed | tf_op | source)
XLA Modules:
  0.0 603.5 jit_solution(9579084468192285088)
XLA Ops:
  0.7 33.3 %all-gather = s32[128,1,100]{2,1,0:T(1,128)S(1)} all-gather(s32[1,1,100]{2,1,0:T(1,128)} %bitcast.97), channel_id=1, replica_groups=mesh['gx'=4,'gy'=4,'gz'=8] {'gx','gy','gz'}, dimensions={0}, use_global_device_ids=true | all-gather | bytes 51600 | tf_op jit(solution)/shard_map/all_gather | solution.py:59
  37.0 8.5 %gather_fusion = bf16[256,128,128]{2,1,0:T(8,128)(2,1)} fusion(bf16[32,128,128]{2,1,0:T(8,128)(2,1)S(1)} %copy-done, s32[1024]{0:T(1024)S(1)} %pad_clamp_fusion.1), kind=kCustom, calls=%fused_computation | custom fusion | bytes 16778240 | tf_op jit(solution)/shard_map/gather | solution.py:70
  45.5 7.4 %broadcast_select_fusion = bf16[128,2,128,128]{3,2,1,0:T(8,128)(2,1)} fusion(bf16[128,2,128,128]{3,2,1,0:T(8,128)(2,1)} %bitcast.85, pred[128,2]{1,0:T(8,128)(4,1)S(1)} %copy.92), kind=kLoop, calls=%fused_computation.10 | loop fusion | flops 4194304 | bytes 16777472 | tf_op jit(solution)/shard_map/jit(_where)/select_n | solution.py:69
  52.9 8.3 %all-to-all-start = ((bf16[128,2,128,128]{3,2,1,0:T(8,128)(2,1)}), bf16[128,2,128,128]{3,2,1,0:T(8,128)(2,1)}, u32[]{:S(2)}, u32[]{:S(2)}) async-start(bf16[128,2,128,128]{3,2,1,0:T(8,128)(2,1)} %broadcast_select_fusion), calls=%async_computation | async-start | bytes 16777216 | tf_op jit(solution)/shard_map/all_to_all | solution.py:48
  64.2 55.5 %collective-permute-done = f32[1,16,16]{2,1,0:T(8,128)S(1)} collective-permute-done((f32[1,16,16]{2,1,0:T(8,128)S(1)}, f32[1,16,16]{2,1,0:T(8,128)S(1)}, u32[]{:S(2)}, u32[]{:S(2)}) %collective-permute-start) | collective-permute-done | bytes 1056 | tf_op jit(solution)/shard_map/ppermute | solution.py:25
  119.7 8.1 %collective-permute-start.2 = (f32[18,1,16]{2,1,0:T(1,128)S(1)}, f32[18,1,16]{2,1,0:T(1,128)S(1)}, u32[]{:S(2)}, u32[]{:S(2)}) collective-permute-start(f32[18,1,16]{2,1,0:T(1,128)S(1)} %get-tuple-element.45), channel_id=1, source_target_pairs={{8,0},{16,8},{24,16},{0,24},{9,1},{17,9},{25,17},{1,25},{10,2},{18... | collective-permute-start | bytes 3464 | tf_op jit(solution)/shard_map/ppermute | solution.py:25
  129.1 14.3 %copy.94 = bf16[4096,1280]{0,1:T(8,128)(2,1)} copy(bf16[4096,1280]{1,0:T(8,128)(2,1)} %bitcast.91) | data formatting | bytes 20971520 | tf_op jit(solution)/shard_map/reshape | solution.py:84
  143.4 10.0 %collective-permute-done.2 = f32[18,1,16]{2,1,0:T(1,128)S(1)} collective-permute-done((f32[18,1,16]{2,1,0:T(1,128)S(1)}, f32[18,1,16]{2,1,0:T(1,128)S(1)}, u32[]{:S(2)}, u32[]{:S(2)}) %collective-permute-start.2) | collective-permute-done | bytes 1184 | tf_op jit(solution)/shard_map/ppermute | solution.py:25
  153.9 13.0 %collective-permute-start.4 = (f32[18,18,1]{2,1,0:T(8,128)S(1)}, f32[18,18,1]{2,1,0:T(8,128)S(1)}, u32[]{:S(2)}, u32[]{:S(2)}) collective-permute-start(f32[18,18,1]{2,1,0:T(8,128)S(1)} %get-tuple-element.34), channel_id=1, source_target_pairs={{1,0},{2,1},{3,2},{4,3},{5,4},{6,5},{7,6},{0,7},{9,8},{10,9},{11,1... | collective-permute-start | bytes 3896 | tf_op jit(solution)/shard_map/ppermute | solution.py:25
  167.0 6.2 %gather_fusion.1 = bf16[100,128,128]{2,1,0:T(8,128)(2,1)} fusion(bf16[256,128,128]{2,1,0:T(8,128)(2,1)} %bitcast.7, s32[1024]{0:T(1024)S(1)} %pad_clamp_fusion), kind=kCustom, calls=%fused_computation.1 | custom fusion | bytes 6554000 | tf_op jit(solution)/shard_map/gather | solution.py:76
  173.1 4.5 copy.97
  177.6 20.5 %fusion.94 = (f32[]{:T(128)}, f32[4096]{0:T(1024)S(1)}) fusion(bf16[4096,1280]{1,0:T(8,128)(2,1)} %bitcast.92, bf16[160,8,10,128]{3,2,1,0:T(8,128)(2,1)S(1)} %bitcast.93, bf16[4096,1280]{0,1:T(8,128)(2,1)} %copy.94), kind=kOutput, calls=%fused_computation.319 | convolution fusion | flops 13442740224 | bytes 24264708 | tf_op jit(solution)/shard_map/dot_general | solution.py:85
  198.1 70.8 %psum.7 = f32[]{:T(128)} all-reduce(f32[]{:T(128)} %get-tuple-element.18), channel_id=1, replica_groups=mesh['gx'=4,'gy'=4,'gz'=8] {'gx','gy','gz'}, use_global_device_ids=true, to_apply=%region_5.6 | all-reduce | flops 1 | bytes 8 | tf_op jit(solution)/shard_map/psum | solution.py:87
  280.0 3.5 collective-permute-done.9
  287.2 3.1 collective-permute-done.11
  305.1 3.1 collective-permute-done.17
  323.3 3.0 collective-permute-done.29
  338.6 3.0 collective-permute-done.35
  353.9 3.0 collective-permute-done.41
  371.9 3.1 collective-permute-done.47
  389.8 3.1 collective-permute-done.53
  393.2 21.2 %fusion.5 = bf16[1280,1280]{0,1:T(8,128)(2,1)} fusion(bf16[16,16,16,1280]{3,2,1,0:T(8,128)(2,1)} %param.4, f32[16,16,16]{2,1,0:T(8,128)S(1)} %fusion.19), kind=kOutput, calls=%fused_computation.12 | convolution fusion | flops 13440778240 | bytes 13778944 | tf_op jit(solution)/shard_map/dot_general | solution.py:108
  414.4 5.7 copy.101
  420.1 7.3 %convert_element_type.36 = bf16[10,128,10,128]{3,2,1,0:T(8,128)(2,1)} reshape(bf16[1280,1280]{1,0:T(8,128)(2,1)} %copy.101) | data formatting | bytes 6553600 | tf_op jit(solution)/shard_map/convert_element_type | solution.py:115
  427.4 5.1 copy.102
  432.5 5.4 broadcast_in_dim.52
  437.9 17.3 %scatter_fusion = bf16[256,128,128]{2,1,0:T(8,128)(2,1)} fusion(bf16[256,128,128]{2,1,0:T(8,128)(2,1)} %broadcast_in_dim.52, s32[100]{0:T(128)S(1)} %fusion.93, bf16[100,128,128]{2,1,0:T(8,128)(2,1)} %bitcast.89), kind=kCustom, calls=%fused_computation.2 | custom fusion | bytes 9830800 | tf_op jit(solution)/shard_map/scatter | solution.py:117
  455.2 6.1 %all-to-all-start.1 = ((bf16[128,2,128,128]{3,2,1,0:T(8,128)(2,1)}), bf16[128,2,128,128]{3,2,1,0:T(8,128)(2,1)}, u32[]{:S(2)}, u32[]{:S(2)}) async-start(bf16[128,2,128,128]{3,2,1,0:T(8,128)(2,1)} %bitcast.84), calls=%async_computation.1 | async-start | bytes 16777216 | tf_op jit(solution)/shard_map/all_to_all | solution.py:48
  461.8 97.5 %all-to-all-done.1 = bf16[128,2,128,128]{3,2,1,0:T(8,128)(2,1)} async-done(((bf16[128,2,128,128]{3,2,1,0:T(8,128)(2,1)}), bf16[128,2,128,128]{3,2,1,0:T(8,128)(2,1)}, u32[]{:S(2)}, u32[]{:S(2)}) %all-to-all-start.1) | async-done | bytes 8388640 | tf_op jit(solution)/shard_map/all_to_all | solution.py:48
  559.3 23.3 %copy.116 = bf16[32,8,128,128]{3,1,2,0:T(8,128)(2,1)} copy(bf16[32,8,128,128]{3,2,1,0:T(8,128)(2,1)} %bitcast.30) | data formatting | bytes 16777216
  582.6 12.1 %copy.103 = bf16[16384,256]{1,0:T(8,128)(2,1)} copy(bf16[16384,256]{0,1:T(8,128)(2,1)} %bitcast.87) | data formatting | bytes 16777216 | tf_op jit(solution)/shard_map/dot_general | solution.py:123
  594.7 5.9 fusion.89
  (180 shorter events, 108.7 us)
Async XLA Ops:
  52.9 114.0 %all-to-all-start = ((bf16[128,2,128,128]{3,2,1,0:T(8,128)(2,1)}), bf16[128,2,128,128]{3,2,1,0:T(8,128)(2,1)}, u32[]{:S(2)}, u32[]{:S(2)}) async-start(bf16[128,2,128,128]{3,2,1,0:T(8,128)(2,1)} %broadcast_select_fusion), calls=%async_computation | async-start | bytes 16777216 | tf_op jit(solution)/shard_map/all_to_all | solution.py:48
  61.2 58.5 %collective-permute-start = (f32[1,16,16]{2,1,0:T(8,128)S(1)}, f32[1,16,16]{2,1,0:T(8,128)S(1)}, u32[]{:S(2)}, u32[]{:S(2)}) collective-permute-start(f32[1,16,16]{2,1,0:T(8,128)S(1)} %broadcast.125), channel_id=1, source_target_pairs={{32,0},{64,32},{96,64},{0,96},{33,1},{65,33},{97,65},{1,97},{34,2}... | collective-permute-start | bytes 3080 | tf_op jit(solution)/shard_map/ppermute | solution.py:25
  64.0 55.7 %collective-permute-start.1 = (f32[1,16,16]{2,1,0:T(8,128)S(1)}, f32[1,16,16]{2,1,0:T(8,128)S(1)}, u32[]{:S(2)}, u32[]{:S(2)}) collective-permute-start(f32[1,16,16]{2,1,0:T(8,128)S(1)} %broadcast.125), channel_id=1, source_target_pairs={{0,32},{32,64},{64,96},{96,0},{1,33},{33,65},{65,97},{97,1},{2,34}... | collective-permute-start | bytes 3080 | tf_op jit(solution)/shard_map/ppermute | solution.py:22
  119.7 33.6 %collective-permute-start.2 = (f32[18,1,16]{2,1,0:T(1,128)S(1)}, f32[18,1,16]{2,1,0:T(1,128)S(1)}, u32[]{:S(2)}, u32[]{:S(2)}) collective-permute-start(f32[18,1,16]{2,1,0:T(1,128)S(1)} %get-tuple-element.45), channel_id=1, source_target_pairs={{8,0},{16,8},{24,16},{0,24},{9,1},{17,9},{25,17},{1,25},{10,2},{18... | collective-permute-start | bytes 3464 | tf_op jit(solution)/shard_map/ppermute | solution.py:25
  127.9 25.8 %collective-permute-start.3 = (f32[18,1,16]{2,1,0:T(1,128)S(1)}, f32[18,1,16]{2,1,0:T(1,128)S(1)}, u32[]{:S(2)}, u32[]{:S(2)}) collective-permute-start(f32[18,1,16]{2,1,0:T(1,128)S(1)} %get-tuple-element.44), channel_id=1, source_target_pairs={{0,8},{8,16},{16,24},{24,0},{1,9},{9,17},{17,25},{25,1},{2,10},{10... | collective-permute-start | bytes 3464 | tf_op jit(solution)/shard_map/ppermute | solution.py:22
  153.9 115.8 %collective-permute-start.4 = (f32[18,18,1]{2,1,0:T(8,128)S(1)}, f32[18,18,1]{2,1,0:T(8,128)S(1)}, u32[]{:S(2)}, u32[]{:S(2)}) collective-permute-start(f32[18,18,1]{2,1,0:T(8,128)S(1)} %get-tuple-element.34), channel_id=1, source_target_pairs={{1,0},{2,1},{3,2},{4,3},{5,4},{6,5},{7,6},{0,7},{9,8},{10,9},{11,1... | collective-permute-start | bytes 3896 | tf_op jit(solution)/shard_map/ppermute | solution.py:25
  166.9 102.8 %collective-permute-start.5 = (f32[18,18,1]{2,1,0:T(8,128)S(1)}, f32[18,18,1]{2,1,0:T(8,128)}, u32[]{:S(2)}, u32[]{:S(2)}) collective-permute-start(f32[18,18,1]{2,1,0:T(8,128)S(1)} %get-tuple-element.35), channel_id=1, source_target_pairs={{0,1},{1,2},{2,3},{3,4},{4,5},{5,6},{6,7},{7,0},{8,9},{9,10},{10,1... | collective-permute-start | bytes 3896 | tf_op jit(solution)/shard_map/ppermute | solution.py:22
  278.7 4.9 collective-permute-start.9
  283.7 6.6 %collective-permute-start.11 = (f32[18,18,1]{2,1,0:T(8,128)S(1)}, f32[18,18,1]{2,1,0:T(8,128)S(1)}, u32[]{:S(2)}, u32[]{:S(2)}) collective-permute-start(f32[18,18,1]{2,1,0:T(8,128)S(1)} %get-tuple-element.33), channel_id=1, source_target_pairs={{0,1},{1,2},{2,3},{3,4},{4,5},{5,6},{6,7},{7,0},{8,9},{9,10},{10,1... | collective-permute-start | bytes 3896 | tf_op jit(solution)/shard_map/ppermute | solution.py:22
  284.2 8.4 %collective-permute-start.18 = (f32[1,8,8]{2,1,0:T(8,128)S(1)}, f32[1,8,8]{2,1,0:T(8,128)S(1)}, u32[]{:S(2)}, u32[]{:S(2)}) collective-permute-start(f32[1,8,8]{2,1,0:T(8,128)S(1)} %broadcast.128), channel_id=1, source_target_pairs={{32,0},{64,32},{96,64},{0,96},{33,1},{65,33},{97,65},{1,97},{34,2}... | collective-permute-start | bytes 776 | tf_op jit(solution)/shard_map/ppermute | solution.py:25
  284.2 8.4 %collective-permute-start.19 = (f32[1,8,8]{2,1,0:T(8,128)S(1)}, f32[1,8,8]{2,1,0:T(8,128)S(1)}, u32[]{:S(2)}, u32[]{:S(2)}) collective-permute-start(f32[1,8,8]{2,1,0:T(8,128)S(1)} %broadcast.128), channel_id=1, source_target_pairs={{0,32},{32,64},{64,96},{96,0},{1,33},{33,65},{65,97},{97,1},{2,34}... | collective-permute-start | bytes 776 | tf_op jit(solution)/shard_map/ppermute | solution.py:22
  290.6 4.9 collective-permute-start.13
  292.7 5.0 collective-permute-start.20
  293.2 4.9 collective-permute-start.21
  296.6 4.9 collective-permute-start.15
  301.6 6.6 %collective-permute-start.17 = (f32[18,18,1]{2,1,0:T(8,128)S(1)}, f32[18,18,1]{2,1,0:T(8,128)S(1)}, u32[]{:S(2)}, u32[]{:S(2)}) collective-permute-start(f32[18,18,1]{2,1,0:T(8,128)S(1)} %get-tuple-element.31), channel_id=1, source_target_pairs={{0,1},{1,2},{2,3},{3,4},{4,5},{5,6},{6,7},{7,0},{8,9},{9,10},{10,1... | collective-permute-start | bytes 3896 | tf_op jit(solution)/shard_map/ppermute | solution.py:22
  302.2 6.7 %collective-permute-start.22 = (f32[10,10,1]{2,1,0:T(8,128)S(1)}, f32[10,10,1]{2,1,0:T(8,128)S(1)}, u32[]{:S(2)}, u32[]{:S(2)}) collective-permute-start(f32[10,10,1]{2,1,0:T(8,128)S(1)} %get-tuple-element.60), channel_id=1, source_target_pairs={{1,0},{2,1},{3,2},{4,3},{5,4},{6,5},{7,6},{0,7},{9,8},{10,9},{11,1... | collective-permute-start | bytes 1208 | tf_op jit(solution)/shard_map/ppermute | solution.py:25
  304.7 5.1 collective-permute-start.23
  316.2 4.9 collective-permute-start.27
  321.2 5.1 collective-permute-start.29
  326.5 4.9 collective-permute-start.31
  331.5 4.9 collective-permute-start.33
  336.5 5.1 collective-permute-start.35
  341.9 4.9 collective-permute-start.37
  346.9 4.9 collective-permute-start.39
  351.9 5.1 collective-permute-start.41
  357.6 4.9 collective-permute-start.43
  363.3 4.9 collective-permute-start.45
  368.4 6.6 %collective-permute-start.47 = (f32[18,18,1]{2,1,0:T(8,128)S(1)}, f32[18,18,1]{2,1,0:T(8,128)S(1)}, u32[]{:S(2)}, u32[]{:S(2)}) collective-permute-start(f32[18,18,1]{2,1,0:T(8,128)S(1)} %get-tuple-element.29), channel_id=1, source_target_pairs={{0,1},{1,2},{2,3},{3,4},{4,5},{5,6},{6,7},{7,0},{8,9},{9,10},{10,1... | collective-permute-start | bytes 3896 | tf_op jit(solution)/shard_map/ppermute | solution.py:22
  381.1 5.0 collective-permute-start.51
  386.4 6.6 %collective-permute-start.53 = (f32[18,18,1]{2,1,0:T(8,128)S(1)}, f32[18,18,1]{2,1,0:T(8,128)S(1)}, u32[]{:S(2)}, u32[]{:S(2)}) collective-permute-start(f32[18,18,1]{2,1,0:T(8,128)S(1)} %get-tuple-element.27), channel_id=1, source_target_pairs={{0,1},{1,2},{2,3},{3,4},{4,5},{5,6},{6,7},{7,0},{8,9},{9,10},{10,1... | collective-permute-start | bytes 3896 | tf_op jit(solution)/shard_map/ppermute | solution.py:22
  455.2 104.1 %all-to-all-start.1 = ((bf16[128,2,128,128]{3,2,1,0:T(8,128)(2,1)}), bf16[128,2,128,128]{3,2,1,0:T(8,128)(2,1)}, u32[]{:S(2)}, u32[]{:S(2)}) async-start(bf16[128,2,128,128]{3,2,1,0:T(8,128)(2,1)} %bitcast.84), calls=%async_computation.1 | async-start | bytes 16777216 | tf_op jit(solution)/shard_map/all_to_all | solution.py:48
  (27 other events, 165.8 us)
where the time goes:
time: 611 us; the launch traced here: 604 us
  waiting for transfers between devices  241 us (39%)
  local copies, waits for them, and re-layouts  115 us (19%)
  blocking collectives  104 us (17%)
  starting transfers between devices  80.2 us (13%)
  matrix products  47.6 us (8%)
  other arithmetic  13.2 us (2%)
    all_to_all x2, waiting for transfers between devices, deliver(): lax.all_to_all(buffer, ('gx', 'gy', 'gz'), split_axis=0, concat_axis=0, t...  97.5 us
    ppermute x27, waiting for transfers between devices, with_halo(): lax.ppermute(lax.slice_in_dim(block, 0, width, axis=dim), axis, backward)  97.4 us
    psum x1, blocking collectives, body(): total = lax.psum(jnp.sum(density), ('gx', 'gy', 'gz'))  70.8 us
    ppermute x27, waiting for transfers between devices, with_halo(): lax.ppermute(lax.slice_in_dim(block, block.shape[dim] - width, None, axis...  46.4 us
    ppermute x27, starting transfers between devices, with_halo(): lax.ppermute(lax.slice_in_dim(block, 0, width, axis=dim), axis, backward)  34.8 us
    all_gather x1, blocking collectives, body(): lax.all_gather(pair_index, ('gx', 'gy', 'gz'), axis=0, tiled=True)  33.3 us
    ppermute x27, starting transfers between devices, with_halo(): lax.ppermute(lax.slice_in_dim(block, block.shape[dim] - width, None, axis...  31 us
    unnamed x8, local copies, waits for them, and re-layouts  25.9 us
  transfers between devices with their start and end apart: 56, of which 47 were waited for; matrix products, arithmetic and copies ran while one was open for 8% of the time, Pallas kernels for 0%

commit v1 on v0

v1 whole, which is shorter than its diff:
```python
import functools

import jax
import jax.numpy as jnp
from jax import lax
from jax.experimental import pallas as pl
from jax.experimental.pallas import tpu as pltpu
from jax.sharding import PartitionSpec as P

MESH = pl.DeviceIdType.MESH
ORB_BLOCKS = 10
NPAIR = 100
BLOCK = 128
HALF = 64
NDEV = 128
NSLOT = 256
NNZ_DEV = 32
CELLS = 4096
LOCAL_ORB = 1280
CHUNK = 256
NCHUNK = CELLS // CHUNK
TOTAL_CELLS = 524288

OMEGA = 0.6
SCREEN = 0.05
FINE = 6.0 + SCREEN
COARSE = 6.0 + 4.0 * SCREEN
NPRE = 2
NCOARSE = 4
NPOST = 2


def constant_response():
    field = 0.0
    for _ in range(NPRE):
        field = field + OMEGA * (1.0 - (FINE - 6.0) * field) / FINE
    rest = 4.0 * (1.0 - (FINE - 6.0) * field)
    correction = 0.0
    for _ in range(NCOARSE):
        correction = correction + OMEGA * (rest - (COARSE - 6.0) * correction) / COARSE
    field = field + correction
    for _ in range(NPOST):
        field = field + OMEGA * (1.0 - (FINE - 6.0) * field) / FINE
    return field


def here():
    z = lax.axis_index("gz")
    return lax.axis_index("gx"), lax.axis_index("gy"), z // 2, z % 2


def beyond(offset):
    x, y, w, c = here()
    dx, dy, dw, dc = offset
    return (x + dx) % 4, (y + dy) % 4, ((w + dw) % 4) * 2 + (c + dc) % 2


def before(offset):
    dx, dy, dw, dc = offset
    return beyond((4 - dx, 4 - dy, 4 - dw, dc))


def offset_of(k):
    return k // 32, (k // 8) % 4, (k // 2) % 4, k % 2


def turn(i):
    a, b, e, c = i % 4, (i // 4) % 4, (i // 16) % 4, (i // 64 + i) % 2
    return a, (a + b) % 4, (a + e) % 4, c


def number(offset):
    dx, dy, dw, dc = offset
    return dx * 32 + dy * 8 + dw * 2 + dc


def remote(src, dst, send, recv, device):
    return pltpu.make_async_remote_copy(
        src_ref=src, dst_ref=dst, send_sem=send, recv_sem=recv,
        device_id=device, device_id_type=MESH,
    )


def beside(v, n, zlane):
    result = []
    for b in range(3):
        total = pltpu.roll(v[b], n, 0) + pltpu.roll(v[b], 48 - n, 0)
        total = total + pltpu.roll(v[b], 16 * n, 1) + pltpu.roll(v[b], 768 - 16 * n, 1)
        up = jnp.where(
            zlane >= 16 - n,
            pltpu.roll(v[(b + 1) % 3], 16 - n, 1),
            pltpu.roll(v[b], 768 - n, 1),
        )
        down = jnp.where(
            zlane < n,
            pltpu.roll(v[(b + 2) % 3], 768 - 16 + n, 1),
            pltpu.roll(v[b], n, 1),
        )
        result.append(total + up + down)
    return result


def pair_sums(r, row, lane):
    r = r + jnp.where(row % 2 == 0, pltpu.roll(r, 47, 0), pltpu.roll(r, 1, 0))
    r = r + jnp.where((lane // 16) % 2 == 0, pltpu.roll(r, 752, 1), pltpu.roll(r, 16, 1))
    return r + jnp.where(lane % 2 == 0, pltpu.roll(r, 767, 1), pltpu.roll(r, 1, 1))


def main_kernel(
    own_ref, blocks_ref, phi_hbm,
    arrived_hbm, pot_ref, table_ref,
    phi, phi_t, sbuf, rbuf_upper, rbuf_lower, lmat, scaled, pieces,
    asked, own_table, own_key, table_s, own_table_s, own_key_s,
    dens, near, source, field, coarse, corr, tz, ty, tx,
    phi_sem, local_sem, ask_send, ask_recv, out_send, out_recv, near_send, near_recv,
    tot_send, tot_recv, back_send, back_recv, self_sem,
):
    rbufs = (rbuf_upper, rbuf_lower)
    x, y, w, c = here()
    me = x * 32 + y * 8 + w * 2 + c

    phi_copy = pltpu.make_async_copy(phi_hbm, phi, phi_sem)
    phi_copy.start()

    axes = (
        [(0, 0, k // 2, k % 2) for k in range(1, 8)],
        [(0, k, 0, 0) for k in range(1, 4)],
        [(k, 0, 0, 0) for k in range(1, 4)],
    )
    barrier = pltpu.get_barrier_semaphore()

    @pl.loop(1, NDEV)
    def _(k):
        pl.semaphore_signal(barrier, inc=1, device_id=beyond(offset_of(k)), device_id_type=MESH)

    asked[0] = jnp.zeros((1, 128), jnp.int32)
    asked[0, :, 0:NPAIR] = own_ref[...]
    lane = lax.broadcasted_iota(jnp.int32, (NDEV, 1, 128), 2)
    own = asked[0:1]
    held = own >> 5
    key = (
        (((x - (held >> 5)) & 3) << 5)
        | (((y - (held >> 3)) & 3) << 3)
        | (((w - (held >> 1)) & 3) << 1)
        | ((c + held) & 1)
    )
    own_key[...] = key
    match = (key == lax.broadcasted_iota(jnp.int32, (NDEV, 1, 128), 0)) & (lane < NPAIR)
    first = jnp.min(jnp.where(match, lane, NPAIR - 1), axis=2, keepdims=True)
    last = jnp.max(jnp.where(match, lane, 0), axis=2, keepdims=True)
    own_table[...] = jnp.where(lane == 0, first, last)
    key_copy = pltpu.make_async_copy(own_key, own_key_s, local_sem.at[0])
    key_copy.start()
    own_copy = pltpu.make_async_copy(own_table, own_table_s, local_sem.at[1])
    own_copy.start()

    pl.semaphore_wait(barrier, NDEV - 1)

    for axis, (offsets, width) in enumerate(zip(axes, (1, 8, 32))):
        for offset in offsets:
            k = number(offset)
            remote(
                asked.at[pl.ds(0, width)], asked.at[pl.ds(k, width)],
                ask_send.at[axis], ask_recv.at[axis], before(offset),
            ).start()
        span = pl.ds(width, len(offsets) * width)
        remote(
            asked.at[span], asked.at[span], ask_send.at[axis], ask_recv.at[axis],
            before(offsets[0]),
        ).wait()

    wanted = asked[...]
    match = ((wanted >> 5) == me) & (lane < NPAIR)
    value = lane * 32 + (wanted & 31)
    first = jnp.min(jnp.where(match, value, 4096), axis=2, keepdims=True)
    last = jnp.max(jnp.where(match, value, -1), axis=2, keepdims=True)
    table = jnp.where(lane == 0, first & 31, last & 31)
    table = jnp.where(lane == 2, (last >= 0).astype(jnp.int32), table)
    table = jnp.where(lane == 3, (last > first).astype(jnp.int32), table)
    table_ref[...] = table
    table_copy = pltpu.make_async_copy(table_ref, table_s, local_sem.at[2])
    table_copy.start()
    table_copy.wait()

    for h in range(2):
        rows = pl.ds(h * HALF, HALF)

        @pl.loop(0, NDEV)
        def _(i):
            offset = turn(i)
            k = number(offset)
            sbuf[h, 2 * k] = blocks_ref[table_s[k, 0, 0], rows, :]
            sbuf[h, 2 * k + 1] = blocks_ref[table_s[k, 0, 1], rows, :]
            span = pl.ds(2 * k, 2)

            @pl.when(k != 0)
            def _():
                remote(
                    sbuf.at[h, span], rbufs[h].at[span], out_send.at[h], out_recv.at[h],
                    beyond(offset),
                ).start()

            @pl.when(k == 0)
            def _():
                rbufs[h][0] = sbuf[h, 0]
                rbufs[h][1] = sbuf[h, 1]

    phi_copy.wait()

    @pl.loop(0, NCHUNK)
    def _(j):
        cells = pl.ds(pl.multiple_of(j * CHUNK, CHUNK), CHUNK)
        for a in range(ORB_BLOCKS):
            phi_t[a * BLOCK:(a + 1) * BLOCK, cells] = phi[cells, a * BLOCK:(a + 1) * BLOCK].T

    key_copy.wait()
    own_copy.wait()
    others = pl.ds(2, NSLOT - 2)
    for h in range(2):
        remote(
            sbuf.at[h, others], rbufs[h].at[others], out_send.at[h], out_recv.at[h],
            beyond((0, 0, 0, 1)),
        ).wait()

        @pl.loop(0, ORB_BLOCKS)
        def _(a):
            rows = pl.ds(pl.multiple_of(a * HALF, HALF), HALF)
            for b in range(ORB_BLOCKS):
                p = a * ORB_BLOCKS + b
                k = own_key_s[0, 0, p]
                slot = 2 * k + (own_table_s[k, 0, 0] != p).astype(jnp.int32)
                lmat[rows, b * BLOCK:(b + 1) * BLOCK] = rbufs[h][slot]

        @pl.loop(0, NCHUNK)
        def _(j):
            cells = pl.ds(pl.multiple_of(j * CHUNK, CHUNK), CHUNK)
            product = jnp.dot(
                lmat[...], phi_t[:, cells], preferred_element_type=jnp.float32
            )
            total = jnp.zeros((HALF, CHUNK), jnp.float32)
            for a in range(ORB_BLOCKS):
                top = a * BLOCK + h * HALF
                total = total + product[a * HALF:(a + 1) * HALF] * phi_t[
                    top:top + HALF, cells
                ].astype(jnp.float32)
            line = jnp.sum(total, axis=0, keepdims=True)
            if h == 0:
                dens[pl.ds(j, 1), :] = line
            else:
                dens[pl.ds(j, 1), :] += line

    spots = [
        (bx, by, bz)
        for bx in range(3) for by in range(3) for bz in range(3)
        if (bx, by, bz) != (1, 1, 1)
    ]
    z = w * 2 + c
    for n, (bx, by, bz) in enumerate(spots):
        remote(
            dens, near.at[n], near_send, near_recv,
            ((x + 5 - bx) % 4, (y + 5 - by) % 4, (z + 9 - bz) % 8),
        ).start()

    tz[0] = jnp.broadcast_to(jnp.sum(dens[...], keepdims=True), (8, 128))

    def spread(axis, held_sums):
        for offset in axes[axis]:
            place = sum(offset) if axis else offset[2] * 2 + offset[3]
            remote(
                held_sums.at[0], held_sums.at[place], tot_send.at[axis], tot_recv.at[axis],
                before(offset),
            ).start()

    def gathered(axis, held_sums):
        span = pl.ds(1, len(axes[axis]))
        remote(
            held_sums.at[span], held_sums.at[span], tot_send.at[axis], tot_recv.at[axis],
            before(axes[axis][0]),
        ).wait()
        return jnp.sum(held_sums[...], axis=0)

    spread(0, tz)
    remote(near, near, near_send, near_recv, beyond((0, 0, 0, 1))).wait()
    source[1, 16:32, 256:512] = dens[...]
    for n, (bx, by, bz) in enumerate(spots):
        source[bz, bx * 16:bx * 16 + 16, by * 256:by * 256 + 256] = near[n]

    row48 = lax.broadcasted_iota(jnp.int32, (48, 768), 0)
    lane48 = lax.broadcasted_iota(jnp.int32, (48, 768), 1)
    zlane = lane48 % 16
    for b in range(3):
        field[b] = (OMEGA / FINE) * source[b]
    for _ in range(NPRE - 1):
        around = beside([field[b] for b in range(3)], 1, zlane)
        for b in range(3):
            field[b] = field[b] + OMEGA * (source[b] - (FINE * field[b] - around[b])) / FINE
    around = beside([field[b] for b in range(3)], 1, zlane)
    for b in range(3):
        rest = source[b] - (FINE * field[b] - around[b])
        coarse[b] = 0.5 * pair_sums(rest, row48, lane48)
        corr[b] = (OMEGA / COARSE) * coarse[b]
    ty[0] = gathered(0, tz)
    spread(1, ty)
    for _ in range(NCOARSE - 1):
        around = beside([corr[b] for b in range(3)], 2, zlane)
        for b in range(3):
            corr[b] = corr[b] + OMEGA * (coarse[b] - (COARSE * corr[b] - around[b])) / COARSE
    tx[0] = gathered(1, ty)
    spread(2, tx)
    for b in range(3):
        field[b] = field[b] + corr[b]
    for _ in range(NPOST):
        around = beside([field[b] for b in range(3)], 1, zlane)
        for b in range(3):
            field[b] = field[b] + OMEGA * (source[b] - (FINE * field[b] - around[b])) / FINE
    total = gathered(2, tx)
    mean = total[0:1, 0:1] * (1.0 / TOTAL_CELLS)
    pot_ref[...] = field[1, 16:32, 256:512] - constant_response() * mean

    for h in range(2):
        rows_in = [a * BLOCK + h * HALF for a in range(ORB_BLOCKS)]

        @pl.loop(0, NCHUNK)
        def _(j):
            cells = pl.ds(pl.multiple_of(j * CHUNK, CHUNK), CHUNK)
            line = pot_ref[pl.ds(j, 1), :]
            for a in range(ORB_BLOCKS):
                scaled[a * HALF:(a + 1) * HALF, cells] = (
                    phi_t[rows_in[a]:rows_in[a] + HALF, cells].astype(jnp.float32) * line
                ).astype(jnp.bfloat16)

        @pl.loop(0, ORB_BLOCKS // 2)
        def _(t):
            columns = pl.ds(pl.multiple_of(t * 2 * BLOCK, 2 * BLOCK), 2 * BLOCK)
            matrix = jnp.dot(
                scaled[...], phi[:, columns], preferred_element_type=jnp.float32
            ) * (CELLS ** -0.5)
            matrix = matrix.astype(jnp.bfloat16)
            for a in range(ORB_BLOCKS):
                for j in range(2):
                    pieces[a * ORB_BLOCKS + 2 * t + j] = matrix[
                        a * HALF:(a + 1) * HALF, j * BLOCK:(j + 1) * BLOCK
                    ]

        @pl.loop(0, NDEV)
        def _(i):
            offset = turn(i)
            k = number(offset)
            sbuf[h, 2 * k] = pieces[own_table_s[k, 0, 0]]
            sbuf[h, 2 * k + 1] = pieces[own_table_s[k, 0, 1]]
            span = pl.ds(2 * k, 2)

            @pl.when(k != 0)
            def _():
                remote(
                    sbuf.at[h, span], arrived_hbm.at[h, span], back_send.at[h], back_recv.at[h],
                    before(offset),
                ).start()

        pltpu.make_async_copy(
            sbuf.at[h, pl.ds(0, 2)], arrived_hbm.at[h, pl.ds(0, 2)], self_sem.at[h]
        ).start()

    for h in range(2):
        pltpu.make_async_copy(
            sbuf.at[h, pl.ds(0, 2)], arrived_hbm.at[h, pl.ds(0, 2)], self_sem.at[h]
        ).wait()
        remote(
            sbuf.at[h, others], arrived_hbm.at[h, others], back_send.at[h], back_recv.at[h],
            beyond((0, 0, 0, 1)),
        ).wait()


GROUP = 32


def add_kernel(table, arrived, out):
    step = pl.program_id(0)

    @pl.when(step == 0)
    def _():
        out[...] = jnp.zeros_like(out)

    @pl.loop(0, GROUP // 2)
    def _(i):
        k = step * (GROUP // 2) + i
        for s in range(2):
            @pl.when(table[k, 0, 2 + s] != 0)
            def _():
                place = table[k, 0, s]
                for h in range(2):
                    out[place, h * HALF:(h + 1) * HALF, :] += arrived[h, 2 * i + s].astype(
                        jnp.float32
                    )


def body(density_blocks, orbital_values, pair_index):
    phi = orbital_values.reshape(CELLS, LOCAL_ORB)
    vmem = pl.BlockSpec(memory_space=pltpu.VMEM)
    anywhere = pl.BlockSpec(memory_space=pl.ANY)
    dma = pltpu.SemaphoreType.DMA
    slots = (2, NSLOT, HALF, BLOCK)
    arrived, pot, table = pl.pallas_call(
        main_kernel,
        out_shape=(
            jax.ShapeDtypeStruct(slots, jnp.bfloat16),
            jax.ShapeDtypeStruct((16, 256), jnp.float32),
            jax.ShapeDtypeStruct((NDEV, 1, 128), jnp.int32),
        ),
        in_specs=[vmem, vmem, anywhere],
        out_specs=(anywhere, vmem, vmem),
        scratch_shapes=[
            pltpu.VMEM((CELLS, LOCAL_ORB), jnp.bfloat16),
            pltpu.VMEM((LOCAL_ORB, CELLS), jnp.bfloat16),
            pltpu.VMEM(slots, jnp.bfloat16),
            pltpu.VMEM(slots[1:], jnp.bfloat16),
            pltpu.VMEM(slots[1:], jnp.bfloat16),
            pltpu.VMEM((ORB_BLOCKS * HALF, LOCAL_ORB), jnp.bfloat16),
            pltpu.VMEM((ORB_BLOCKS * HALF, CELLS), jnp.bfloat16),
            pltpu.VMEM((NPAIR, HALF, BLOCK), jnp.bfloat16),
            pltpu.VMEM((NDEV, 1, 128), jnp.int32),
            pltpu.VMEM((NDEV, 1, 128), jnp.int32),
            pltpu.VMEM((1, 1, 128), jnp.int32),
            pltpu.SMEM((NDEV, 1, 128), jnp.int32),
            pltpu.SMEM((NDEV, 1, 128), jnp.int32),
            pltpu.SMEM((1, 1, 128), jnp.int32),
            pltpu.VMEM((16, 256), jnp.float32),
            pltpu.VMEM((26, 16, 256), jnp.float32),
            pltpu.VMEM((3, 48, 768), jnp.float32),
            pltpu.VMEM((3, 48, 768), jnp.float32),
            pltpu.VMEM((3, 48, 768), jnp.float32),
            pltpu.VMEM((3, 48, 768), jnp.float32),
            pltpu.VMEM((8, 8, 128), jnp.float32),
            pltpu.VMEM((4, 8, 128), jnp.float32),
            pltpu.VMEM((4, 8, 128), jnp.float32),
            dma, dma((3,)), dma((3,)), dma((3,)), dma((2,)), dma((2,)), dma, dma,
            dma((3,)), dma((3,)), dma((2,)), dma((2,)), dma((2,)),
        ],
        compiler_params=pltpu.CompilerParams(
            collective_id=0, has_side_effects=True, vmem_limit_bytes=60 * 2**20
        ),
        cost_estimate=pl.CostEstimate(
            flops=4 * CELLS * LOCAL_ORB * LOCAL_ORB, bytes_accessed=40 * 2**20, transcendentals=0
        ),
        name="collocate_solve_integrate",
    )(pair_index, density_blocks, phi)
    summed = pl.pallas_call(
        add_kernel,
        grid=(NSLOT // GROUP,),
        out_shape=jax.ShapeDtypeStruct((NNZ_DEV, BLOCK, BLOCK), jnp.float32),
        in_specs=[
            pl.BlockSpec(memory_space=pltpu.SMEM),
            pl.BlockSpec((2, GROUP, HALF, BLOCK), lambda i: (0, i, 0, 0)),
        ],
        out_specs=pl.BlockSpec((NNZ_DEV, BLOCK, BLOCK), lambda i: (0, 0, 0)),
        compiler_params=pltpu.CompilerParams(vmem_limit_bytes=32 * 2**20),
        name="add_arrived",
    )(table, arrived)
    return summed, pot.reshape(16, 16, 16)


def solution(mesh):
    return jax.shard_map(
        body,
        mesh=mesh,
        in_specs=(
            P(("gx", "gy", "gz"), None, None),
            P("gx", "gy", "gz", None),
            P(("gx", "gy", "gz"), None),
        ),
        out_specs=(P(("gx", "gy", "gz"), None, None), P("gx", "gy", "gz")),
        check_vma=False,
    )
```

time: 611 us -> 264 us (0.43); the launches traced: 604 us -> 263 us
  Pallas kernels: 0 us -> 258 us
  waiting for transfers between devices: 241 us -> 0 us
  local copies, waits for them, and re-layouts: 115 us -> 4.97 us
  blocking collectives: 104 us -> 0 us
  starting transfers between devices: 80.2 us -> 0 us
  matrix products: 47.6 us -> 0 us
  other arithmetic: 13.2 us -> 0 us
    pallas_call x0 -> x2, Pallas kernels: none -> 258 us  [the longest x1 250 us: body(): pl.pallas_call(main_kernel, out_shape=(jax.ShapeDtypeStruct(slots, jnp.bf...]
    ppermute x54 -> x0, waiting for transfers between devices: 144 us -> none  [the longest x27 97.4 us: with_halo(): lax.ppermute(lax.slice_in_dim(block, 0, width, axis=dim), axis, backward)]
    all_to_all x2 -> x0, waiting for transfers between devices: 97.5 us -> none  [deliver(): lax.all_to_all(buffer, ('gx', 'gy', 'gz'), split_axis=0, concat_axis=0, t...]
    psum x1 -> x0, blocking collectives: 70.8 us -> none  [body(): total = lax.psum(jnp.sum(density), ('gx', 'gy', 'gz'))]
    ppermute x54 -> x0, starting transfers between devices: 65.8 us -> none  [the longest x27 34.8 us: with_halo(): lax.ppermute(lax.slice_in_dim(block, 0, width, axis=dim), axis, backward)]
    dot_general x3 -> x0, matrix products: 47.6 us -> none  [the longest x1 21.2 us: body(): lax.dot_general(orbitals, weighted, (((0,), (0,)), ((), ())), preferred_e...]
    all_gather x1 -> x0, blocking collectives: 33.3 us -> none  [body(): lax.all_gather(pair_index, ('gx', 'gy', 'gz'), axis=0, tiled=True)]
    unnamed x8 -> x6, local copies, waits for them, and re-layouts: 25.9 us -> 4.22 us
  transfers between devices with their start and end apart: 56 -> 0, of which waited for: 47 -> 0; matrix products, arithmetic and copies ran while one was open for 8% -> 0% of each run, Pallas kernels for 0% -> 0%
where the time goes in v1:
time: 264 us; the launch traced here: 263 us
  Pallas kernels  258 us (98%)
  local copies, waits for them, and re-layouts  4.97 us (2%)
    pallas_call x1, Pallas kernels, body(): pl.pallas_call(main_kernel, out_shape=(jax.ShapeDtypeStruct(slots, jnp.bf...  250 us
    pallas_call x1, Pallas kernels, body(): pl.pallas_call(add_kernel, grid=(NSLOT // GROUP,), out_shape=jax.ShapeDty...  7.51 us

profile of v1, /device:TPU:0, one launch (start us, length us, event | category | flops | bytes accessed | tf_op | source)
XLA Modules:
  0.0 263.2 jit_solution(7120606730568336780)
XLA Ops:
  0.6 250.0 %collocate_solve_integrate.1 = (bf16[2,256,64,128]{3,2,1,0:T(8,128)(2,1)}, f32[16,256]{1,0:T(8,128)}, s32[128,1,128]{2,1,0:T(1,128)}) custom-call(s32[1,100]{1,0:T(1,128)} %own_ref.1, bf16[32,128,128]{2,1,0:T(8,128)(2,1)} %blocks_ref.1, bf16[4096,1280]{1,0:T(8,128)(2,1)} %bitcast.1), custom_call_target="tpu_custom_call" | custom-call | flops 26843545600 | bytes 41943040 | tf_op jit(solution)/shard_map/collocate_solve_integrate/pallas_call | solution.py:403
  250.7 0.0 copy-start
  250.7 3.4 %copy-done = bf16[2,256,64,128]{3,2,1,0:T(8,128)(2,1)S(1)} copy-done((bf16[2,256,64,128]{3,2,1,0:T(8,128)(2,1)S(1)}, bf16[2,256,64,128]{3,2,1,0:T(8,128)(2,1)}, u32[]{:S(2)}) %copy-start) | copy-done | bytes 8388632
  254.0 0.0 copy-start.1
  254.0 0.8 copy-done.1
  254.9 0.0 copy-start.2
  254.9 7.5 %add_arrived.1 = f32[32,128,128]{2,1,0:T(8,128)} custom-call(s32[128,1,128]{2,1,0:T(1,128)S(1)} %copy-done.1, bf16[2,256,64,128]{3,2,1,0:T(8,128)(2,1)S(1)} %copy-done), custom_call_target="tpu_custom_call" | custom-call | tf_op jit(solution)/shard_map/add_arrived/pallas_call | solution.py:447
  262.4 0.0 copy-done.2
  262.4 0.8 reshape.11
Async XLA Ops:
  250.7 3.4 %copy-start = (bf16[2,256,64,128]{3,2,1,0:T(8,128)(2,1)S(1)}, bf16[2,256,64,128]{3,2,1,0:T(8,128)(2,1)}, u32[]{:S(2)}) copy-start(bf16[2,256,64,128]{3,2,1,0:T(8,128)(2,1)} %get-tuple-element.6.arrived) | copy-start | bytes 25165828
  254.0 0.8 copy-start.1
  254.9 7.5 %copy-start.2 = (f32[16,256]{1,0:T(8,128)S(1)}, f32[16,256]{1,0:T(8,128)}, u32[]{:S(2)}) copy-start(f32[16,256]{1,0:T(8,128)} %get-tuple-element.7) | copy-start | bytes 49156

commit v2 on v1

v2 whole, which is shorter than its diff:
```python
import functools

import jax
import jax.numpy as jnp
from jax import lax
from jax.experimental import pallas as pl
from jax.experimental.pallas import tpu as pltpu
from jax.sharding import PartitionSpec as P

MESH = pl.DeviceIdType.MESH
ORB_BLOCKS = 10
NPAIR = 100
BLOCK = 128
QUARTER = 32
NDEV = 128
NPLANE = 32
NSLOT = 256
NNZ_DEV = 32
CELLS = 4096
LOCAL_ORB = 1280
CHUNK = 256
NCHUNK = CELLS // CHUNK
TOTAL_CELLS = 524288
PARTS = ((0, (32, 16)), (48, (32, 16)), (96, (16, 16)))
ROUND_ROWS = (80, 48)

OMEGA = 0.6
SCREEN = 0.05
FINE = 6.0 + SCREEN
COARSE = 6.0 + 4.0 * SCREEN
NPRE = 2
NCOARSE = 4
NPOST = 2


def constant_response():
    field = 0.0
    for _ in range(NPRE):
        field = field + OMEGA * (1.0 - (FINE - 6.0) * field) / FINE
    rest = 4.0 * (1.0 - (FINE - 6.0) * field)
    correction = 0.0
    for _ in range(NCOARSE):
        correction = correction + OMEGA * (rest - (COARSE - 6.0) * correction) / COARSE
    field = field + correction
    for _ in range(NPOST):
        field = field + OMEGA * (1.0 - (FINE - 6.0) * field) / FINE
    return field


def here():
    z = lax.axis_index("gz")
    return lax.axis_index("gx"), lax.axis_index("gy"), z // 2, z % 2


def beyond(offset):
    x, y, w, c = here()
    dx, dy, dw, dc = offset
    return (x + dx) % 4, (y + dy) % 4, ((w + dw) % 4) * 2 + (c + dc) % 2


def before(offset):
    dx, dy, dw, dc = offset
    return beyond((4 - dx, 4 - dy, 4 - dw, dc))


def offset_of(k):
    return k // 32, (k // 8) % 4, (k // 2) % 4, k % 2


def turn(i):
    a, b, e, c = i % 4, (i // 4) % 4, (i // 16) % 4, (i // 64 + i) % 2
    return a, (a + b) % 4, (a + e) % 4, c


def plane_turn(axis, i):
    a, b, c = i % 4, (i // 4) % 4, (i // 16 + i) % 2
    u, v = ((a + b) % 4, a) if axis == 1 else (a, (a + b) % 4)
    return u * 8 + v * 2 + c


def plane_offset(axis, t):
    u, v, c = t // 8, (t // 2) % 4, t % 2
    return ((0, u, v, c), (u, 0, v, c), (u, v, 0, c))[axis]


def along(axis, j):
    return tuple(j if n == axis else 0 for n in range(3)) + (0,)


def number(offset):
    dx, dy, dw, dc = offset
    return dx * 32 + dy * 8 + dw * 2 + dc


def remote(src, dst, send, recv, device):
    return pltpu.make_async_remote_copy(
        src_ref=src, dst_ref=dst, send_sem=send, recv_sem=recv,
        device_id=device, device_id_type=MESH,
    )


def beside(v, n):
    rows, lanes = v[0].shape
    zlane = lax.broadcasted_iota(jnp.int32, (rows, lanes), 1) % 16
    result = []
    for b in range(3):
        total = pltpu.roll(v[b], n, 0) + pltpu.roll(v[b], rows - n, 0)
        total = total + pltpu.roll(v[b], 16 * n, 1) + pltpu.roll(v[b], lanes - 16 * n, 1)
        up = jnp.where(
            zlane >= 16 - n,
            pltpu.roll(v[(b + 1) % 3], 16 - n, 1),
            pltpu.roll(v[b], lanes - n, 1),
        )
        down = jnp.where(
            zlane < n,
            pltpu.roll(v[(b + 2) % 3], lanes - 16 + n, 1),
            pltpu.roll(v[b], n, 1),
        )
        result.append(total + up + down)
    return result


def pair_sums(r):
    rows, lanes = r.shape
    row = lax.broadcasted_iota(jnp.int32, r.shape, 0)
    lane = lax.broadcasted_iota(jnp.int32, r.shape, 1)
    r = r + jnp.where(row % 2 == 0, pltpu.roll(r, rows - 1, 0), pltpu.roll(r, 1, 0))
    r = r + jnp.where(
        (lane // 16) % 2 == 0, pltpu.roll(r, lanes - 16, 1), pltpu.roll(r, 16, 1)
    )
    return r + jnp.where(lane % 2 == 0, pltpu.roll(r, lanes - 1, 1), pltpu.roll(r, 1, 1))


def first_last(match, value, low, high):
    first = jnp.min(jnp.where(match, value, high), axis=1, keepdims=True)
    last = jnp.max(jnp.where(match, value, low), axis=1, keepdims=True)
    return first, last


def main_kernel(
    own_ref, blocks_ref, phi_hbm,
    arrived_hbm, pot_ref, table_ref,
    phi, phi_t,
    ag_a, ag_b, ag_c,
    s0a, s0b, s0c, s1a, s1b, s1c,
    r0a, r0b, r0c, r1a, r1b, r1c,
    lmat0, lmat1, scaled, pieces,
    asked, own_table, own_key, send_table, own_table_s, own_key_s, send_table_s, place_s,
    dens, near, source, pre, field, coarse, corr, tz, ty, tx,
    phi_sem, local_sem, ask_send, ask_recv, ag_send, ag_recv, out_send, out_recv,
    near_send, near_recv, tot_send, tot_recv, back_send, back_recv, self_sem,
):
    gathered_blocks = (ag_a, ag_b, ag_c)
    sbufs = ((s0a, s0b, s0c), (s1a, s1b, s1c))
    rbufs = ((r0a, r0b, r0c), (r1a, r1b, r1c))
    lmats = (lmat0, lmat1)
    x, y, w, c = here()
    me = x * 32 + y * 8 + w * 2 + c

    phi_copy = pltpu.make_async_copy(phi_hbm, phi, phi_sem)
    phi_copy.start()

    axes = (
        [(0, 0, k // 2, k % 2) for k in range(1, 8)],
        [(0, k, 0, 0) for k in range(1, 4)],
        [(k, 0, 0, 0) for k in range(1, 4)],
    )
    barrier = pltpu.get_barrier_semaphore()
    for offsets in axes:
        for offset in offsets:
            pl.semaphore_signal(barrier, inc=1, device_id=beyond(offset), device_id_type=MESH)

    asked[0] = jnp.zeros((1, 128), jnp.int32)
    asked[0, :, 0:NPAIR] = own_ref[...]
    lane = lax.broadcasted_iota(jnp.int32, (NDEV, 128), 1)
    row = lax.broadcasted_iota(jnp.int32, (NDEV, 128), 0)
    own = asked[0]
    held = own >> 5
    key = (
        (((x - (held >> 5)) & 3) << 5)
        | (((y - (held >> 3)) & 3) << 3)
        | (((w - (held >> 1)) & 3) << 1)
        | ((c + held) & 1)
    )
    own_key[...] = key
    first, last = first_last((key == row) & (lane < NPAIR), lane, 0, NPAIR - 1)
    own_table[...] = jnp.where(lane == 0, first, last)
    key_copy = pltpu.make_async_copy(own_key, own_key_s, local_sem.at[0])
    key_copy.start()
    own_copy = pltpu.make_async_copy(own_table, own_table_s, local_sem.at[1])
    own_copy.start()
    for axis, (top, rounds) in enumerate(PARTS):
        gathered_blocks[axis][0:NNZ_DEV] = blocks_ref[:, top:top + sum(rounds), :]

    pl.semaphore_wait(barrier, 13)

    for axis, (offsets, width) in enumerate(zip(axes, (1, 8, 32))):
        for offset in offsets:
            k = number(offset)
            remote(
                asked.at[pl.ds(0, width)], asked.at[pl.ds(k, width)],
                ask_send.at[axis], ask_recv.at[axis], before(offset),
            ).start()
        if axis == 0:
            for j in (1, 3, 2):
                for part, (top, rounds) in enumerate(PARTS):
                    remote(
                        blocks_ref.at[:, pl.ds(top, sum(rounds)), :],
                        gathered_blocks[part].at[pl.ds(j * NNZ_DEV, NNZ_DEV)],
                        ag_send.at[part], ag_recv.at[part], before(along(part, j)),
                    ).start()
        span = pl.ds(width, len(offsets) * width)
        remote(
            asked.at[span], asked.at[span], ask_send.at[axis], ask_recv.at[axis],
            before(offsets[0]),
        ).wait()

    wanted = asked[:, 0, :]
    asks = (
        wanted[0:32],
        jnp.concatenate([wanted[n * 32:n * 32 + 8] for n in range(4)], axis=0),
        wanted,
    )
    for axis, base in enumerate((0, 32, 64)):
        ask = asks[axis]
        count = ask.shape[0]
        lane_n = lane[0:count]
        value = lane_n * 32 + (ask & 31)
        table = jnp.zeros((count, 128), jnp.int32)
        for j in range(4):
            holder = (
                ((x + j) % 4) * 32 + y * 8 + w * 2 + c,
                x * 32 + ((y + j) % 4) * 8 + w * 2 + c,
                x * 32 + y * 8 + ((w + j) % 4) * 2 + c,
            )[axis]
            first, last = first_last(
                ((ask >> 5) == holder) & (lane_n < NPAIR), value, 0, NNZ_DEV * 128 - 1
            )
            table = jnp.where(lane_n == 2 * j, j * NNZ_DEV + (first & 31), table)
            table = jnp.where(lane_n == 2 * j + 1, j * NNZ_DEV + (last & 31), table)
        send_table[base:base + count] = table
    table_copy = pltpu.make_async_copy(send_table, send_table_s, local_sem.at[2])
    table_copy.start()
    table_copy.wait()
    for part in range(3):
        span = pl.ds(NNZ_DEV, 3 * NNZ_DEV)
        remote(
            gathered_blocks[part].at[span], gathered_blocks[part].at[span],
            ag_send.at[part], ag_recv.at[part], before(along(part, 1)),
        ).wait()

    for r in range(2):
        @pl.loop(0, NPLANE)
        def _(i):
            for part, (top, rounds) in enumerate(PARTS):
                t = plane_turn(part, i)
                rows = pl.ds(sum(rounds[:r]), rounds[r])
                line = (t, 32 + t, 64 + (t // 8) * 32 + ((t // 2) % 4) * 8 + t % 2)[part]
                send, recv = sbufs[r][part], rbufs[r][part]
                for n in range(8):
                    send[8 * t + n] = gathered_blocks[part][send_table_s[line, n], rows, :]
                span = pl.ds(8 * t, 8)

                @pl.when(t != 0)
                def _():
                    remote(
                        send.at[span], recv.at[span], out_send.at[r, part], out_recv.at[r, part],
                        beyond(plane_offset(part, t)),
                    ).start()

                @pl.when(t == 0)
                def _():
                    for n in range(8):
                        recv[n] = send[n]

    key_copy.wait()
    own_copy.wait()

    @pl.loop(0, NPAIR)
    def _(p):
        k = own_key_s[0, p]
        rank = (own_table_s[k, 0] != p).astype(jnp.int32)
        dx, dy, dw = k >> 5, (k >> 3) & 3, (k >> 1) & 3
        place_s[0, p] = (k & 31) * 8 + ((4 - dx) & 3) * 2 + rank
        place_s[1, p] = (dx * 8 + (k & 7)) * 8 + ((4 - dy) & 3) * 2 + rank
        place_s[2, p] = (dx * 8 + dy * 2 + (k & 1)) * 8 + ((4 - dw) & 3) * 2 + rank

    first, last = first_last(
        ((wanted >> 5) == me) & (lane < NPAIR), lane * 32 + (wanted & 31), -1, NNZ_DEV * 128
    )
    table = jnp.where(lane == 0, first & 31, last & 31)
    table = jnp.where(lane == 2, (last >= 0).astype(jnp.int32), table)
    table = jnp.where(lane == 3, (last > first).astype(jnp.int32), table)
    table_ref[...] = table

    phi_copy.wait()

    @pl.loop(0, NCHUNK)
    def _(j):
        cells = pl.ds(pl.multiple_of(j * CHUNK, CHUNK), CHUNK)
        for a in range(ORB_BLOCKS):
            phi_t[a * BLOCK:(a + 1) * BLOCK, cells] = phi[cells, a * BLOCK:(a + 1) * BLOCK].T

    spots = [
        (bx, by, bz)
        for bx in range(3) for by in range(3) for bz in range(3)
        if (bx, by, bz) != (1, 1, 1)
    ]
    z = w * 2 + c

    def send_density(part):
        for n, (bx, by, bz) in enumerate(spots):
            remote(
                dens.at[pl.ds(8 * part, 8)], near.at[part, n],
                near_send.at[part], near_recv.at[part],
                ((x + 5 - bx) % 4, (y + 5 - by) % 4, (z + 9 - bz) % 8),
            ).start()

    for r in range(2):
        for part in range(3):
            others = pl.ds(8, NSLOT - 8)
            remote(
                sbufs[r][part].at[others], rbufs[r][part].at[others],
                out_send.at[r, part], out_recv.at[r, part], beyond(along(2, 1)),
            ).wait()

        @pl.loop(0, ORB_BLOCKS)
        def _(a):
            for b in range(ORB_BLOCKS):
                into = 0
                for part, (top, rounds) in enumerate(PARTS):
                    rows = pl.ds(pl.multiple_of(a * ROUND_ROWS[r] + into, 16), rounds[r])
                    lmats[r][rows, b * BLOCK:(b + 1) * BLOCK] = rbufs[r][part][
                        place_s[part, a * ORB_BLOCKS + b]
                    ]
                    into += rounds[r]

        def collocate(j):
            cells = pl.ds(pl.multiple_of(j * CHUNK, CHUNK), CHUNK)
            product = jnp.dot(
                lmats[r][...], phi_t[:, cells], preferred_element_type=jnp.float32
            )
            total = jnp.zeros((16, CHUNK), jnp.float32)
            for a in range(ORB_BLOCKS):
                into = a * ROUND_ROWS[r]
                for part, (top, rounds) in enumerate(PARTS):
                    start = a * BLOCK + top + sum(rounds[:r])
                    for n in range(0, rounds[r], 16):
                        total = total + product[into + n:into + n + 16] * phi_t[
                            start + n:start + n + 16, cells
                        ].astype(jnp.float32)
                    into += rounds[r]
            line = jnp.sum(total, axis=0, keepdims=True)
            if r == 0:
                dens[pl.ds(j, 1), :] = line
            else:
                dens[pl.ds(j, 1), :] += line

        if r == 0:
            pl.loop(0, NCHUNK)(collocate)
        else:
            pl.loop(0, NCHUNK // 2)(collocate)
            send_density(0)
            pl.loop(NCHUNK // 2, NCHUNK)(collocate)
            send_density(1)

    tz[0] = jnp.broadcast_to(jnp.sum(dens[...], keepdims=True), (8, 128))

    def spread(axis, held_sums):
        for offset in axes[axis]:
            place = sum(offset) if axis else offset[2] * 2 + offset[3]
            remote(
                held_sums.at[0], held_sums.at[place], tot_send.at[axis], tot_recv.at[axis],
                before(offset),
            ).start()

    def gathered(axis, held_sums):
        span = pl.ds(1, len(axes[axis]))
        remote(
            held_sums.at[span], held_sums.at[span], tot_send.at[axis], tot_recv.at[axis],
            before(axes[axis][0]),
        ).wait()
        return jnp.sum(held_sums[...], axis=0)

    spread(0, tz)
    source[1, 16:32, 256:512] = dens[...]
    for part in range(2):
        remote(
            near.at[part], near.at[part], near_send.at[part], near_recv.at[part],
            beyond((0, 0, 0, 1)),
        ).wait()
        for n, (bx, by, bz) in enumerate(spots):
            top = bx * 16 + part * 8
            source[bz, top:top + 8, by * 256:by * 256 + 256] = near[part, n]

    inner = (slice(8, 40), slice(128, 640))
    slabs = range(3)
    gain, keep = OMEGA / FINE, 1.0 - OMEGA
    wide = [source[b] for b in slabs]
    around = beside([gain * v for v in wide], 1)
    for b in slabs:
        pre[b] = (keep * gain + gain) * wide[b] + gain * around[b]
    wide = [pre[b] for b in slabs]
    around = beside(wide, 1)
    for b in slabs:
        rest = source[(b,) + inner] - FINE * wide[b][inner] + around[b][inner]
        coarse[b] = (0.5 * OMEGA / COARSE) * pair_sums(rest)
        corr[b] = coarse[b]
    ty[0] = gathered(0, tz)
    spread(1, ty)
    for _ in range(NCOARSE - 1):
        around = beside([corr[b] for b in slabs], 2)
        for b in slabs:
            corr[b] = keep * corr[b] + coarse[b] + (OMEGA / COARSE) * around[b]
    tx[0] = gathered(1, ty)
    spread(2, tx)
    for b in slabs:
        field[b] = pre[(b,) + inner] + corr[b]
    for _ in range(NPOST):
        around = beside([field[b] for b in slabs], 1)
        for b in slabs:
            field[b] = keep * field[b] + gain * (source[(b,) + inner] + around[b])
    total = gathered(2, tx)
    mean = total[0:1, 0:1] * (1.0 / TOTAL_CELLS)
    pot_ref[...] = field[1, 8:24, 128:384] - constant_response() * mean

    returning = (s0a, s0b, r0a, r0b)
    for q, send in enumerate(returning):
        rows_in = [a * BLOCK + q * QUARTER for a in range(ORB_BLOCKS)]

        @pl.loop(0, NCHUNK)
        def _(j):
            cells = pl.ds(pl.multiple_of(j * CHUNK, CHUNK), CHUNK)
            line = pot_ref[pl.ds(j, 1), :]
            for a in range(ORB_BLOCKS):
                scaled[a * QUARTER:(a + 1) * QUARTER, cells] = (
                    phi_t[rows_in[a]:rows_in[a] + QUARTER, cells].astype(jnp.float32) * line
                ).astype(jnp.bfloat16)

        @pl.loop(0, ORB_BLOCKS // 2)
        def _(t):
            columns = pl.ds(pl.multiple_of(t * 2 * BLOCK, 2 * BLOCK), 2 * BLOCK)
            matrix = jnp.dot(
                scaled[...], phi[:, columns], preferred_element_type=jnp.float32
            ) * (CELLS ** -0.5)
            matrix = matrix.astype(jnp.bfloat16)
            for a in range(ORB_BLOCKS):
                for j in range(2):
                    pieces[a * ORB_BLOCKS + 2 * t + j] = matrix[
                        a * QUARTER:(a + 1) * QUARTER, j * BLOCK:(j + 1) * BLOCK
                    ]

        @pl.loop(0, NDEV)
        def _(i):
            offset = turn(i)
            k = number(offset)
            send[2 * k] = pieces[own_table_s[k, 0]]
            send[2 * k + 1] = pieces[own_table_s[k, 1]]
            span = pl.ds(2 * k, 2)

            @pl.when(k != 0)
            def _():
                remote(
                    send.at[span], arrived_hbm.at[q, span], back_send.at[q], back_recv.at[q],
                    before(offset),
                ).start()

        pltpu.make_async_copy(
            send.at[pl.ds(0, 2)], arrived_hbm.at[q, pl.ds(0, 2)], self_sem.at[q]
        ).start()

    for q, send in enumerate(returning):
        pltpu.make_async_copy(
            send.at[pl.ds(0, 2)], arrived_hbm.at[q, pl.ds(0, 2)], self_sem.at[q]
        ).wait()
        others = pl.ds(2, NSLOT - 2)
        remote(
            send.at[others], arrived_hbm.at[q, others], back_send.at[q], back_recv.at[q],
            beyond((0, 0, 0, 1)),
        ).wait()


def add_kernel(table, arrived, out, buf, sems):
    def fetch(k):
        span = pl.ds(2 * k, 2)
        return pltpu.make_async_copy(arrived.at[:, span], buf.at[:, span], sems.at[k])

    @pl.loop(0, NDEV)
    def _(k):
        @pl.when(table[k, 2] != 0)
        def _():
            fetch(k).start()

    out[...] = jnp.zeros_like(out)

    @pl.loop(0, NDEV)
    def _(k):
        @pl.when(table[k, 2] != 0)
        def _():
            fetch(k).wait()
        for s in range(2):
            @pl.when(table[k, 2 + s] != 0)
            def _():
                place = table[k, s]
                for q in range(4):
                    out[place, q * QUARTER:(q + 1) * QUARTER, :] += buf[q, 2 * k + s].astype(
                        jnp.float32
                    )


def body(density_blocks, orbital_values, pair_index):
    phi = orbital_values.reshape(CELLS, LOCAL_ORB)
    vmem = pl.BlockSpec(memory_space=pltpu.VMEM)
    smem = pl.BlockSpec(memory_space=pltpu.SMEM)
    anywhere = pl.BlockSpec(memory_space=pl.ANY)
    dma = pltpu.SemaphoreType.DMA
    slots = (4, NSLOT, QUARTER, BLOCK)
    bf16, f32, i32 = jnp.bfloat16, jnp.float32, jnp.int32
    transit = [
        pltpu.VMEM((NSLOT, rounds[r], BLOCK), bf16) for r in range(2) for top, rounds in PARTS
    ]
    arrived, pot, table = pl.pallas_call(
        main_kernel,
        out_shape=(
            jax.ShapeDtypeStruct(slots, bf16),
            jax.ShapeDtypeStruct((16, 256), f32),
            jax.ShapeDtypeStruct((NDEV, 128), i32),
        ),
        in_specs=[vmem, vmem, anywhere],
        out_specs=(anywhere, vmem, vmem),
        scratch_shapes=[
            pltpu.VMEM((CELLS, LOCAL_ORB), bf16),
            pltpu.VMEM((LOCAL_ORB, CELLS), bf16),
        ] + [
            pltpu.VMEM((4 * NNZ_DEV, sum(rounds), BLOCK), bf16) for top, rounds in PARTS
        ] + transit + transit + [
            pltpu.VMEM((ORB_BLOCKS * ROUND_ROWS[0], LOCAL_ORB), bf16),
            pltpu.VMEM((ORB_BLOCKS * ROUND_ROWS[1], LOCAL_ORB), bf16),
            pltpu.VMEM((ORB_BLOCKS * QUARTER, CELLS), bf16),
            pltpu.VMEM((NPAIR, QUARTER, BLOCK), bf16),
            pltpu.VMEM((NDEV, 1, 128), i32),
            pltpu.VMEM((NDEV, 128), i32),
            pltpu.VMEM((1, 128), i32),
            pltpu.VMEM((192, 128), i32),
            pltpu.SMEM((NDEV, 128), i32),
            pltpu.SMEM((1, 128), i32),
            pltpu.SMEM((192, 128), i32),
            pltpu.SMEM((3, 128), i32),
            pltpu.VMEM((16, 256), f32),
            pltpu.VMEM((2, 26, 8, 256), f32),
            pltpu.VMEM((3, 48, 768), f32),
            pltpu.VMEM((3, 48, 768), f32),
            pltpu.VMEM((3, 32, 512), f32),
            pltpu.VMEM((3, 32, 512), f32),
            pltpu.VMEM((3, 32, 512), f32),
            pltpu.VMEM((8, 8, 128), f32),
            pltpu.VMEM((4, 8, 128), f32),
            pltpu.VMEM((4, 8, 128), f32),
            dma, dma((3,)), dma((3,)), dma((3,)), dma((3,)), dma((3,)), dma((2, 3)), dma((2, 3)),
            dma((2,)), dma((2,)), dma((3,)), dma((3,)), dma((4,)), dma((4,)), dma((4,)),
        ],
        compiler_params=pltpu.CompilerParams(
            collective_id=0, has_side_effects=True, vmem_limit_bytes=60 * 2**20
        ),
        cost_estimate=pl.CostEstimate(
            flops=4 * CELLS * LOCAL_ORB * LOCAL_ORB, bytes_accessed=40 * 2**20, transcendentals=0
        ),
        name="collocate_solve_integrate",
    )(pair_index, density_blocks, phi)
    summed = pl.pallas_call(
        add_kernel,
        out_shape=jax.ShapeDtypeStruct((NNZ_DEV, BLOCK, BLOCK), f32),
        in_specs=[smem, anywhere],
        out_specs=vmem,
        scratch_shapes=[pltpu.VMEM(slots, bf16), dma((NDEV,))],
        compiler_params=pltpu.CompilerParams(vmem_limit_bytes=60 * 2**20),
        name="add_arrived",
    )(table, arrived)
    return summed, pot.reshape(16, 16, 16)


def solution(mesh):
    return jax.shard_map(
        body,
        mesh=mesh,
        in_specs=(
            P(("gx", "gy", "gz"), None, None),
            P("gx", "gy", "gz", None),
            P(("gx", "gy", "gz"), None),
        ),
        out_specs=(P(("gx", "gy", "gz"), None, None), P("gx", "gy", "gz")),
        check_vma=False,
    )
```

time: 264 us -> 240 us (0.909)
  Pallas kernels: 258 us -> 238 us
  local copies, waits for them, and re-layouts: 4.97 us -> 0.76 us
    pallas_call x2, Pallas kernels: 258 us -> 238 us  [the longest x1 228 us: body(): pl.pallas_call(main_kernel, out_shape=(jax.ShapeDtypeStruct(slots, bf16),...]
    unnamed x6 -> x2, local copies, waits for them, and re-layouts: 4.22 us -> 0.01 us
where the time goes in v2:
time: 240 us; the launch traced here: 239 us
  Pallas kernels  238 us (99%)
    pallas_call x1, Pallas kernels, body(): pl.pallas_call(main_kernel, out_shape=(jax.ShapeDtypeStruct(slots, bf16),...  228 us
    pallas_call x1, Pallas kernels, body(): pl.pallas_call(add_kernel, out_shape=jax.ShapeDtypeStruct((NNZ_DEV, BLOCK...  9.78 us

profile of v2, /device:TPU:0, one launch (start us, length us, event | category | flops | bytes accessed | tf_op | source)
XLA Modules:
  0.0 239.3 jit_solution(10609831679993192005)
XLA Ops:
  0.6 228.1 %collocate_solve_integrate.1 = (bf16[4,256,32,128]{3,2,1,0:T(8,128)(2,1)}, f32[16,256]{1,0:T(8,128)}, s32[128,128]{1,0:T(8,128)}) custom-call(s32[1,100]{1,0:T(1,128)} %own_ref.1, bf16[32,128,128]{2,1,0:T(8,128)(2,1)} %blocks_ref.1, bf16[4096,1280]{1,0:T(8,128)(2,1)} %bitcast.1), custom_call_target="tpu_custom_call" | custom-call | flops 26843545600 | bytes 41943040 | tf_op jit(solution)/shard_map/collocate_solve_integrate/pallas_call | solution.py:522
  228.7 0.0 copy-start
  228.7 9.8 %add_arrived.1 = f32[32,128,128]{2,1,0:T(8,128)} custom-call(s32[128,128]{1,0:T(8,128)} %get-tuple-element.5.table, bf16[4,256,32,128]{3,2,1,0:T(8,128)(2,1)} %get-tuple-element.6.arrived), custom_call_target="tpu_custom_call" | custom-call | tf_op jit(solution)/shard_map/add_arrived/pallas_call | solution.py:570
  238.5 0.0 copy-done
  238.5 0.8 reshape.11
Async XLA Ops:
  228.7 9.8 %copy-start = (f32[16,256]{1,0:T(8,128)S(1)}, f32[16,256]{1,0:T(8,128)}, u32[]{:S(2)}) copy-start(f32[16,256]{1,0:T(8,128)} %get-tuple-element.7) | copy-start | bytes 49156

commit v3 on v2

--- a/solution.py
+++ b/solution.py
@@ -21,8 +21,9 @@
 CHUNK = 256
 NCHUNK = CELLS // CHUNK
 TOTAL_CELLS = 524288
-PARTS = ((0, (32, 16)), (48, (32, 16)), (96, (16, 16)))
-ROUND_ROWS = (80, 48)
+GROUP = 16
+PARTS = ((0, 16, 32), (48, 64, 80), (96, 112, 32))
+ROUND_TOPS = ((0, 16, 48, 64, 96, 112), (32, 80))
 
 OMEGA = 0.6
 SCREEN = 0.05
@@ -139,20 +140,20 @@
 
 def main_kernel(
     own_ref, blocks_ref, phi_hbm,
-    arrived_hbm, pot_ref, table_ref,
+    out_ref, pot_ref,
     phi, phi_t,
     ag_a, ag_b, ag_c,
-    s0a, s0b, s0c, s1a, s1b, s1c,
-    r0a, r0b, r0c, r1a, r1b, r1c,
-    lmat0, lmat1, scaled, pieces,
-    asked, own_table, own_key, send_table, own_table_s, own_key_s, send_table_s, place_s,
+    s0a, s0b, s0c, s1,
+    r0a, r0b, r0c, r1,
+    lmat0, lmat1, scaled, pieces, sums,
+    asked, own_table, own_key, send_table, order,
+    own_table_s, own_key_s, send_table_s, place_s, order_s,
     dens, near, source, pre, field, coarse, corr, tz, ty, tx,
     phi_sem, local_sem, ask_send, ask_recv, ag_send, ag_recv, out_send, out_recv,
-    near_send, near_recv, tot_send, tot_recv, back_send, back_recv, self_sem,
+    near_send, near_recv, tot_send, tot_recv, back_send, back_recv,
 ):
     gathered_blocks = (ag_a, ag_b, ag_c)
-    sbufs = ((s0a, s0b, s0c), (s1a, s1b, s1c))
-    rbufs = ((r0a, r0b, r0c), (r1a, r1b, r1c))
+    sbufs, rbufs = (s0a, s0b, s0c, s1), (r0a, r0b, r0c, r1)
     lmats = (lmat0, lmat1)
     x, y, w, c = here()
     me = x * 32 + y * 8 + w * 2 + c
@@ -189,8 +190,9 @@
     key_copy.start()
     own_copy = pltpu.make_async_copy(own_table, own_table_s, local_sem.at[1])
     own_copy.start()
-    for axis, (top, rounds) in enumerate(PARTS):
-        gathered_blocks[axis][0:NNZ_DEV] = blocks_ref[:, top:top + sum(rounds), :]
+    for part, tops in enumerate(PARTS):
+        for n, top in enumerate(tops):
+            gathered_blocks[part][n, 0:NNZ_DEV] = blocks_ref[:, top:top + GROUP, :]
 
     pl.semaphore_wait(barrier, 13)
 
@@ -201,14 +203,13 @@
                 asked.at[pl.ds(0, width)], asked.at[pl.ds(k, width)],
                 ask_send.at[axis], ask_recv.at[axis], before(offset),
             ).start()
-        if axis == 0:
-            for j in (1, 3, 2):
-                for part, (top, rounds) in enumerate(PARTS):
-                    remote(
-                        blocks_ref.at[:, pl.ds(top, sum(rounds)), :],
-                        gathered_blocks[part].at[pl.ds(j * NNZ_DEV, NNZ_DEV)],
-                        ag_send.at[part], ag_recv.at[part], before(along(part, j)),
-                    ).start()
+        for j in (1, 3, 2):
+            for part, tops in enumerate(PARTS):
+                remote(
+                    blocks_ref.at[:, pl.ds(tops[axis], GROUP), :],
+                    gathered_blocks[part].at[axis, pl.ds(j * NNZ_DEV, NNZ_DEV)],
+                    ag_send.at[part], ag_recv.at[part], before(along(part, j)),
+                ).start()
         span = pl.ds(width, len(offsets) * width)
         remote(
             asked.at[span], asked.at[span], ask_send.at[axis], ask_recv.at[axis],
@@ -245,21 +246,30 @@
     for part in range(3):
         span = pl.ds(NNZ_DEV, 3 * NNZ_DEV)
         remote(
-            gathered_blocks[part].at[span], gathered_blocks[part].at[span],
+            gathered_blocks[part].at[:, span], gathered_blocks[part].at[:, span],
             ag_send.at[part], ag_recv.at[part], before(along(part, 1)),
         ).wait()
 
-    for r in range(2):
+    def send_round(r):
         @pl.loop(0, NPLANE)
         def _(i):
-            for part, (top, rounds) in enumerate(PARTS):
+            for part in range(3):
                 t = plane_turn(part, i)
-                rows = pl.ds(sum(rounds[:r]), rounds[r])
                 line = (t, 32 + t, 64 + (t // 8) * 32 + ((t // 2) % 4) * 8 + t % 2)[part]
-                send, recv = sbufs[r][part], rbufs[r][part]
-                for n in range(8):
-                    send[8 * t + n] = gathered_blocks[part][send_table_s[line, n], rows, :]
-                span = pl.ds(8 * t, 8)
+                if r == 0:
+                    send, recv, base, count = sbufs[part], rbufs[part], 8 * t, 8
+                    for n in range(8):
+                        block = send_table_s[line, n]
+                        for g in range(2):
+                            send[base + n, g * GROUP:(g + 1) * GROUP] = gathered_blocks[part][g, block]
+                else:
+                    send, recv = s1, r1
+                    base = (4 * t, 128 + 8 * t, 384 + 4 * t)[part]
+                    slots = ((0, 2, 4, 6), range(8), (1, 3, 5, 7))[part]
+                    count = len(slots)
+                    for n, slot in enumerate(slots):
+                        send[base + n] = gathered_blocks[part][2, send_table_s[line, slot]]
+                span = pl.ds(base, count)
 
                 @pl.when(t != 0)
                 def _():
@@ -270,8 +280,11 @@
 
                 @pl.when(t == 0)
                 def _():
-                    for n in range(8):
-                        recv[n] = send[n]
+                    for n in range(count):
+                        recv[base + n] = send[base + n]
+
+    send_round(0)
+    send_round(1)
 
     key_copy.wait()
     own_copy.wait()
@@ -284,14 +297,35 @@
         place_s[0, p] = (k & 31) * 8 + ((4 - dx) & 3) * 2 + rank
         place_s[1, p] = (dx * 8 + (k & 7)) * 8 + ((4 - dy) & 3) * 2 + rank
         place_s[2, p] = (dx * 8 + dy * 2 + (k & 1)) * 8 + ((4 - dw) & 3) * 2 + rank
+        place_s[3, p] = rank
 
     first, last = first_last(
         ((wanted >> 5) == me) & (lane < NPAIR), lane * 32 + (wanted & 31), -1, NNZ_DEV * 128
     )
-    table = jnp.where(lane == 0, first & 31, last & 31)
-    table = jnp.where(lane == 2, (last >= 0).astype(jnp.int32), table)
-    table = jnp.where(lane == 3, (last > first).astype(jnp.int32), table)
-    table_ref[...] = table
+    blocks = [
+        jnp.where(last >= 0, first & 31, NNZ_DEV), jnp.where(last > first, last & 31, NNZ_DEV)
+    ]
+    slots = [2 * row[:, 0:1], 2 * row[:, 0:1] + 1]
+    keys = [block * NSLOT + slot for block, slot in zip(blocks, slots)]
+    across = [jnp.broadcast_to(key, (NDEV, 128)).T for key in keys]
+    ranks = [
+        sum(jnp.sum((other < key).astype(jnp.int32), axis=1, keepdims=True) for other in across)
+        for key in keys
+    ]
+    for n in range(2):
+        at = [rank == lane + 128 * n for rank in ranks]
+        order[n:n + 1] = sum(
+            jnp.sum(jnp.where(a, slot, 0), axis=0, keepdims=True) for a, slot in zip(at, slots)
+        )
+        order[2 + n:3 + n] = sum(
+            jnp.sum(jnp.where(a, block, 0), axis=0, keepdims=True) for a, block in zip(at, blocks)
+        )
+    order[4:5] = sum(
+        jnp.sum((block <= lane).astype(jnp.int32), axis=0, keepdims=True) for block in blocks
+    )
+    order[5:8] = jnp.zeros((3, 128), jnp.int32)
+    order_copy = pltpu.make_async_copy(order, order_s, local_sem.at[3])
+    order_copy.start()
 
     phi_copy.wait()
 
@@ -318,38 +352,46 @@
 
     for r in range(2):
         for part in range(3):
-            others = pl.ds(8, NSLOT - 8)
+            if r == 0:
+                send, recv, span = sbufs[part], rbufs[part], pl.ds(8, NSLOT - 8)
+            else:
+                send, recv = s1, r1
+                span = (pl.ds(4, 124), pl.ds(136, 248), pl.ds(388, 124))[part]
             remote(
-                sbufs[r][part].at[others], rbufs[r][part].at[others],
+                send.at[span], recv.at[span],
                 out_send.at[r, part], out_recv.at[r, part], beyond(along(2, 1)),
             ).wait()
+
+        high = GROUP * len(ROUND_TOPS[r])
 
         @pl.loop(0, ORB_BLOCKS)
         def _(a):
             for b in range(ORB_BLOCKS):
-                into = 0
-                for part, (top, rounds) in enumerate(PARTS):
-                    rows = pl.ds(pl.multiple_of(a * ROUND_ROWS[r] + into, 16), rounds[r])
-                    lmats[r][rows, b * BLOCK:(b + 1) * BLOCK] = rbufs[r][part][
-                        place_s[part, a * ORB_BLOCKS + b]
-                    ]
-                    into += rounds[r]
+                p = a * ORB_BLOCKS + b
+                columns = slice(b * BLOCK, (b + 1) * BLOCK)
+                if r == 0:
+                    for part in range(3):
+                        rows = pl.ds(pl.multiple_of(a * high + part * 2 * GROUP, GROUP), 2 * GROUP)
+                        lmat0[rows, columns] = rbufs[part][place_s[part, p]]
+                else:
+                    rank = place_s[3, p]
+                    one = r1[(place_s[0, p] >> 1) + rank * (384 + (place_s[2, p] >> 1) - (place_s[0, p] >> 1))]
+                    two = r1[128 + place_s[1, p]]
+                    lmat1[pl.ds(pl.multiple_of(a * high, GROUP), GROUP), columns] = one
+                    lmat1[pl.ds(pl.multiple_of(a * high + GROUP, GROUP), GROUP), columns] = two
 
         def collocate(j):
             cells = pl.ds(pl.multiple_of(j * CHUNK, CHUNK), CHUNK)
             product = jnp.dot(
                 lmats[r][...], phi_t[:, cells], preferred_element_type=jnp.float32
             )
-            total = jnp.zeros((16, CHUNK), jnp.float32)
+            total = jnp.zeros((GROUP, CHUNK), jnp.float32)
             for a in range(ORB_BLOCKS):
-                into = a * ROUND_ROWS[r]
-                for part, (top, rounds) in enumerate(PARTS):
-                    start = a * BLOCK + top + sum(rounds[:r])
-                    for n in range(0, rounds[r], 16):
-                        total = total + product[into + n:into + n + 16] * phi_t[
-                            start + n:start + n + 16, cells
-                        ].astype(jnp.float32)
-                    into += rounds[r]
+                for n, top in enumerate(ROUND_TOPS[r]):
+                    into, start = a * high + n * GROUP, a * BLOCK + top
+                    total = total + product[into:into + GROUP] * phi_t[
+                        start:start + GROUP, cells
+                    ].astype(jnp.float32)
             line = jnp.sum(total, axis=0, keepdims=True)
             if r == 0:
                 dens[pl.ds(j, 1), :] = line
@@ -424,8 +466,8 @@
     mean = total[0:1, 0:1] * (1.0 / TOTAL_CELLS)
     pot_ref[...] = field[1, 8:24, 128:384] - constant_response() * mean
 
-    returning = (s0a, s0b, r0a, r0b)
-    for q, send in enumerate(returning):
+    for q in range(4):
+        send, arrived, per = sbufs[q], rbufs[q], (2, 2, 2, 4)[q]
         rows_in = [a * BLOCK + q * QUARTER for a in range(ORB_BLOCKS)]
 
         @pl.loop(0, NCHUNK)
@@ -454,98 +496,99 @@
         def _(i):
             offset = turn(i)
             k = number(offset)
-            send[2 * k] = pieces[own_table_s[k, 0]]
-            send[2 * k + 1] = pieces[own_table_s[k, 1]]
-            span = pl.ds(2 * k, 2)
+            for s in range(2):
+                block = pieces[own_table_s[k, s]]
+                if q < 3:
+                    send[2 * k + s] = block
+                else:
+                    send[4 * k + 2 * s] = block[:GROUP]
+                    send[4 * k + 2 * s + 1] = block[GROUP:]
+            span = pl.ds(per * k, per)
 
             @pl.when(k != 0)
             def _():
                 remote(
-                    send.at[span], arrived_hbm.at[q, span], back_send.at[q], back_recv.at[q],
+                    send.at[span], arrived.at[span], back_send.at[q], back_recv.at[q],
                     before(offset),
                 ).start()
 
-        pltpu.make_async_copy(
-            send.at[pl.ds(0, 2)], arrived_hbm.at[q, pl.ds(0, 2)], self_sem.at[q]
-        ).start()
-
-    for q, send in enumerate(returning):
-        pltpu.make_async_copy(
-            send.at[pl.ds(0, 2)], arrived_hbm.at[q, pl.ds(0, 2)], self_sem.at[q]
-        ).wait()
-        others = pl.ds(2, NSLOT - 2)
+            @pl.when(k == 0)
+            def _():
+                for n in range(per):
+                    arrived[n] = send[n]
+
+    order_copy.wait()
+    for q in range(4):
+        send, arrived, per = sbufs[q], rbufs[q], (2, 2, 2, 4)[q]
+        others = pl.ds(per, per * (NDEV - 1))
         remote(
-            send.at[others], arrived_hbm.at[q, others], back_send.at[q], back_recv.at[q],
+            send.at[others], arrived.at[others], back_send.at[q], back_recv.at[q],
             beyond((0, 0, 0, 1)),
         ).wait()
 
-
-def add_kernel(table, arrived, out, buf, sems):
-    def fetch(k):
-        span = pl.ds(2 * k, 2)
-        return pltpu.make_async_copy(arrived.at[:, span], buf.at[:, span], sems.at[k])
-
-    @pl.loop(0, NDEV)
-    def _(k):
-        @pl.when(table[k, 2] != 0)
-        def _():
-            fetch(k).start()
-
-    out[...] = jnp.zeros_like(out)
-
-    @pl.loop(0, NDEV)
-    def _(k):
-        @pl.when(table[k, 2] != 0)
-        def _():
-            fetch(k).wait()
-        for s in range(2):
-            @pl.when(table[k, 2 + s] != 0)
-            def _():
-                place = table[k, s]
-                for q in range(4):
-                    out[place, q * QUARTER:(q + 1) * QUARTER, :] += buf[q, 2 * k + s].astype(
-                        jnp.float32
-                    )
+        def add(n, carry):
+            previous, run = carry
+            slot, block = order_s[n // 128, n % 128], order_s[2 + n // 128, n % 128]
+            if q < 3:
+                value = arrived[slot].astype(jnp.float32)
+            else:
+                value = jnp.concatenate(
+                    [arrived[2 * slot], arrived[2 * slot + 1]], axis=0
+                ).astype(jnp.float32)
+            run = run * (block == previous).astype(jnp.float32) + value
+            sums[n] = run
+            return block, run
+
+        lax.fori_loop(
+            0, NSLOT, add, (jnp.int32(-1), jnp.zeros((QUARTER, BLOCK), jnp.float32)), unroll=4
+        )
+
+        @pl.loop(0, NNZ_DEV)
+        def _(n):
+            stop = order_s[4, n]
+            start = jnp.where(n == 0, 0, order_s[4, jnp.maximum(n - 1, 0)])
+            some = (stop > start).astype(jnp.float32)
+            out_ref[n, q * QUARTER:(q + 1) * QUARTER, :] = sums[jnp.maximum(stop - 1, 0)] * some
 
 
 def body(density_blocks, orbital_values, pair_index):
     phi = orbital_values.reshape(CELLS, LOCAL_ORB)
     vmem = pl.BlockSpec(memory_space=pltpu.VMEM)
-    smem = pl.BlockSpec(memory_space=pltpu.SMEM)
     anywhere = pl.BlockSpec(memory_space=pl.ANY)
     dma = pltpu.SemaphoreType.DMA
-    slots = (4, NSLOT, QUARTER, BLOCK)
     bf16, f32, i32 = jnp.bfloat16, jnp.float32, jnp.int32
-    transit = [
-        pltpu.VMEM((NSLOT, rounds[r], BLOCK), bf16) for r in range(2) for top, rounds in PARTS
+    transit = [pltpu.VMEM((NSLOT, 2 * GROUP, BLOCK), bf16)] * 3 + [
+        pltpu.VMEM((2 * NSLOT, GROUP, BLOCK), bf16)
     ]
-    arrived, pot, table = pl.pallas_call(
+    summed, pot = pl.pallas_call(
         main_kernel,
         out_shape=(
-            jax.ShapeDtypeStruct(slots, bf16),
+            jax.ShapeDtypeStruct((NNZ_DEV, BLOCK, BLOCK), f32),
             jax.ShapeDtypeStruct((16, 256), f32),
-            jax.ShapeDtypeStruct((NDEV, 128), i32),
         ),
         in_specs=[vmem, vmem, anywhere],
-        out_specs=(anywhere, vmem, vmem),
+        out_specs=(vmem, vmem),
         scratch_shapes=[
             pltpu.VMEM((CELLS, LOCAL_ORB), bf16),
             pltpu.VMEM((LOCAL_ORB, CELLS), bf16),
         ] + [
-            pltpu.VMEM((4 * NNZ_DEV, sum(rounds), BLOCK), bf16) for top, rounds in PARTS
+            pltpu.VMEM((3, 4 * NNZ_DEV, GROUP, BLOCK), bf16) for _ in PARTS
         ] + transit + transit + [
-            pltpu.VMEM((ORB_BLOCKS * ROUND_ROWS[0], LOCAL_ORB), bf16),
-            pltpu.VMEM((ORB_BLOCKS * ROUND_ROWS[1], LOCAL_ORB), bf16),
+            pltpu.VMEM((ORB_BLOCKS * GROUP * len(tops), LOCAL_ORB), bf16) for tops in ROUND_TOPS
+        ] + [
             pltpu.VMEM((ORB_BLOCKS * QUARTER, CELLS), bf16),
             pltpu.VMEM((NPAIR, QUARTER, BLOCK), bf16),
+            pltpu.VMEM((NSLOT, QUARTER, BLOCK), f32),
             pltpu.VMEM((NDEV, 1, 128), i32),
             pltpu.VMEM((NDEV, 128), i32),
             pltpu.VMEM((1, 128), i32),
             pltpu.VMEM((192, 128), i32),
+            pltpu.VMEM((8, 128), i32),
             pltpu.SMEM((NDEV, 128), i32),
             pltpu.SMEM((1, 128), i32),
             pltpu.SMEM((192, 128), i32),
-            pltpu.SMEM((3, 128), i32),
+            pltpu.SMEM((4, 128), i32),
+            pltpu.SMEM((8, 128), i32),
             pltpu.VMEM((16, 256), f32),
             pltpu.VMEM((2, 26, 8, 256), f32),
             pltpu.VMEM((3, 48, 768), f32),
@@ -556,26 +599,17 @@
             pltpu.VMEM((8, 8, 128), f32),
             pltpu.VMEM((4, 8, 128), f32),
             pltpu.VMEM((4, 8, 128), f32),
-            dma, dma((3,)), dma((3,)), dma((3,)), dma((3,)), dma((3,)), dma((2, 3)), dma((2, 3)),
-            dma((2,)), dma((2,)), dma((3,)), dma((3,)), dma((4,)), dma((4,)), dma((4,)),
+            dma, dma((4,)), dma((3,)), dma((3,)), dma((3,)), dma((3,)), dma((2, 3)), dma((2, 3)),
+            dma((2,)), dma((2,)), dma((3,)), dma((3,)), dma((4,)), dma((4,)),
         ],
         compiler_params=pltpu.CompilerParams(
-            collective_id=0, has_side_effects=True, vmem_limit_bytes=60 * 2**20
+            collective_id=0, has_side_effects=True, vmem_limit_bytes=61 * 2**20
         ),
         cost_estimate=pl.CostEstimate(
             flops=4 * CELLS * LOCAL_ORB * LOCAL_ORB, bytes_accessed=40 * 2**20, transcendentals=0
         ),
         name="collocate_solve_integrate",
     )(pair_index, density_blocks, phi)
-    summed = pl.pallas_call(
-        add_kernel,
-        out_shape=jax.ShapeDtypeStruct((NNZ_DEV, BLOCK, BLOCK), f32),
-        in_specs=[smem, anywhere],
-        out_specs=vmem,
-        scratch_shapes=[pltpu.VMEM(slots, bf16), dma((NDEV,))],
-        compiler_params=pltpu.CompilerParams(vmem_limit_bytes=60 * 2**20),
-        name="add_arrived",
-    )(table, arrived)
     return summed, pot.reshape(16, 16, 16)
 
 

time: 240 us -> 229 us (0.954)
  Pallas kernels: 238 us -> 223 us
  local copies, waits for them, and re-layouts: 0.76 us -> 4.6 us
    pallas_call x2 -> x1, Pallas kernels: 238 us -> 223 us  [body(): pl.pallas_call(main_kernel, out_shape=(jax.ShapeDtypeStruct((NNZ_DEV, BLO...]
    unnamed x2 -> x1, local copies, waits for them, and re-layouts: 0.01 us -> 3.13 us
where the time goes in v3:
time: 229 us; the launch traced here: 228 us
  Pallas kernels  223 us (97%)
  local copies, waits for them, and re-layouts  4.6 us (2%)
    pallas_call x1, Pallas kernels, body(): pl.pallas_call(main_kernel, out_shape=(jax.ShapeDtypeStruct((NNZ_DEV, BLO...  223 us

profile of v3, /device:TPU:0, one launch (start us, length us, event | category | flops | bytes accessed | tf_op | source)
XLA Modules:
  0.0 228.5 jit_solution(6265220088124187114)
XLA Ops:
  0.6 223.2 %collocate_solve_integrate.1 = (f32[32,128,128]{2,1,0:T(8,128)}, f32[16,256]{1,0:T(8,128)}) custom-call(s32[1,100]{1,0:T(1,128)} %own_ref.1, bf16[32,128,128]{2,1,0:T(8,128)(2,1)} %blocks_ref.1, bf16[4096,1280]{1,0:T(8,128)(2,1)} %bitcast.1), custom_call_target="tpu_custom_call" | custom-call | flops 26843545600 | bytes 41943040 | tf_op jit(solution)/shard_map/collocate_solve_integrate/pallas_call | solution.py:563
  223.9 1.5 reshape.11
  225.3 3.1 %copy.6 = f32[32,128,128]{2,1,0:T(8,128)} copy(f32[32,128,128]{2,1,0:T(8,128)} %get-tuple-element.8) | data formatting | bytes 4194304

commit v4 on v3

--- a/solution.py
+++ b/solution.py
@@ -11,7 +11,6 @@
 ORB_BLOCKS = 10
 NPAIR = 100
 BLOCK = 128
-QUARTER = 32
 NDEV = 128
 NPLANE = 32
 NSLOT = 256
@@ -22,8 +21,11 @@
 NCHUNK = CELLS // CHUNK
 TOTAL_CELLS = 524288
 GROUP = 16
+PIECES = ((0, 16), (16, 32), (48, 32), (80, 16), (96, 16), (112, 16))
+EARLY = 26
 PARTS = ((0, 16, 32), (48, 64, 80), (96, 112, 32))
-ROUND_TOPS = ((0, 16, 48, 64, 96, 112), (32, 80))
+ROUND_TOPS = ((0, 48, 96), (16, 64, 112), (32, 80))
+
 
 OMEGA = 0.6
 SCREEN = 0.05
@@ -143,18 +145,18 @@
     out_ref, pot_ref,
     phi, phi_t,
     ag_a, ag_b, ag_c,
-    s0a, s0b, s0c, s1,
-    r0a, r0b, r0c, r1,
-    lmat0, lmat1, scaled, pieces, sums,
+    s0, s0c, s1, s1c, s2,
+    r0, r0c, r1, r1c, r2,
+    lmat0, lmat1, lmat2, scaled, pieces, sums,
     asked, own_table, own_key, send_table, order,
     own_table_s, own_key_s, send_table_s, place_s, order_s,
     dens, near, source, pre, field, coarse, corr, tz, ty, tx,
-    phi_sem, local_sem, ask_send, ask_recv, ag_send, ag_recv, out_send, out_recv,
+    phi_sem, local_sem, ask_send, ask_recv, ag_send, ag_recv, pass_recv, out_send, out_recv,
     near_send, near_recv, tot_send, tot_recv, back_send, back_recv,
 ):
     gathered_blocks = (ag_a, ag_b, ag_c)
-    sbufs, rbufs = (s0a, s0b, s0c, s1), (r0a, r0b, r0c, r1)
-    lmats = (lmat0, lmat1)
+    sbufs, rbufs = ((s0, s0c), (s1, s1c), (s2,)), ((r0, r0c), (r1, r1c), (r2,))
+    lmats = (lmat0, lmat1, lmat2)
     x, y, w, c = here()
     me = x * 32 + y * 8 + w * 2 + c
 
@@ -173,28 +175,22 @@
 
     asked[0] = jnp.zeros((1, 128), jnp.int32)
     asked[0, :, 0:NPAIR] = own_ref[...]
-    lane = lax.broadcasted_iota(jnp.int32, (NDEV, 128), 1)
-    row = lax.broadcasted_iota(jnp.int32, (NDEV, 128), 0)
-    own = asked[0]
-    held = own >> 5
-    key = (
-        (((x - (held >> 5)) & 3) << 5)
-        | (((y - (held >> 3)) & 3) << 3)
-        | (((w - (held >> 1)) & 3) << 1)
-        | ((c + held) & 1)
-    )
-    own_key[...] = key
-    first, last = first_last((key == row) & (lane < NPAIR), lane, 0, NPAIR - 1)
-    own_table[...] = jnp.where(lane == 0, first, last)
-    key_copy = pltpu.make_async_copy(own_key, own_key_s, local_sem.at[0])
-    key_copy.start()
-    own_copy = pltpu.make_async_copy(own_table, own_table_s, local_sem.at[1])
-    own_copy.start()
-    for part, tops in enumerate(PARTS):
-        for n, top in enumerate(tops):
-            gathered_blocks[part][n, 0:NNZ_DEV] = blocks_ref[:, top:top + GROUP, :]
-
     pl.semaphore_wait(barrier, 13)
+
+    def pass_on(n):
+        half = NNZ_DEV // 2
+        for part in range(3):
+            for way, j in enumerate((1, 3)):
+                held = pl.ds(j * NNZ_DEV, NNZ_DEV)
+                remote(
+                    gathered_blocks[part].at[n, held], gathered_blocks[part].at[n, held],
+                    ag_send.at[part], ag_recv.at[n, part, way], before(along(part, 1)),
+                ).wait_recv()
+                remote(
+                    gathered_blocks[part].at[n, pl.ds(j * NNZ_DEV + way * half, half)],
+                    gathered_blocks[part].at[n, pl.ds(2 * NNZ_DEV + way * half, half)],
+                    ag_send.at[part], pass_recv.at[part], before(along(part, j)),
+                ).start()
 
     for axis, (offsets, width) in enumerate(zip(axes, (1, 8, 32))):
         for offset in offsets:
@@ -203,18 +199,46 @@
                 asked.at[pl.ds(0, width)], asked.at[pl.ds(k, width)],
                 ask_send.at[axis], ask_recv.at[axis], before(offset),
             ).start()
-        for j in (1, 3, 2):
+        if axis == 0:
+            for n in range(3):
+                for part, tops in enumerate(PARTS):
+                    for way, j in enumerate((1, 3)):
+                        remote(
+                            blocks_ref.at[:, pl.ds(tops[n], GROUP), :],
+                            gathered_blocks[part].at[n, pl.ds(j * NNZ_DEV, NNZ_DEV)],
+                            ag_send.at[part], ag_recv.at[n, part, way], before(along(part, j)),
+                        ).start()
+        else:
+            pass_on(axis - 1)
+        if axis == 0:
+            lane = lax.broadcasted_iota(jnp.int32, (NDEV, 128), 1)
+            row = lax.broadcasted_iota(jnp.int32, (NDEV, 128), 0)
+            own = asked[0]
+            held = own >> 5
+            key = (
+                (((x - (held >> 5)) & 3) << 5)
+                | (((y - (held >> 3)) & 3) << 3)
+                | (((w - (held >> 1)) & 3) << 1)
+                | ((c + held) & 1)
+            )
+            own_key[...] = key
+            first, last = first_last((key == row) & (lane < NPAIR), lane, 0, NPAIR - 1)
+            own_table[...] = jnp.where(lane == 0, first, last)
+            key_copy = pltpu.make_async_copy(own_key, own_key_s, local_sem.at[0])
+            key_copy.start()
+            own_copy = pltpu.make_async_copy(own_table, own_table_s, local_sem.at[1])
+            own_copy.start()
+        elif axis == 1:
             for part, tops in enumerate(PARTS):
-                remote(
-                    blocks_ref.at[:, pl.ds(tops[axis], GROUP), :],
-                    gathered_blocks[part].at[axis, pl.ds(j * NNZ_DEV, NNZ_DEV)],
-                    ag_send.at[part], ag_recv.at[part], before(along(part, j)),
-                ).start()
+                for n, top in enumerate(tops):
+                    gathered_blocks[part][n, 0:NNZ_DEV] = blocks_ref[:, top:top + GROUP, :]
         span = pl.ds(width, len(offsets) * width)
         remote(
             asked.at[span], asked.at[span], ask_send.at[axis], ask_recv.at[axis],
             before(offsets[0]),
         ).wait()
+
+    pass_on(2)
 
     wanted = asked[:, 0, :]
     asks = (
@@ -244,47 +268,66 @@
     table_copy.start()
     table_copy.wait()
     for part in range(3):
-        span = pl.ds(NNZ_DEV, 3 * NNZ_DEV)
+        sent = pl.ds(NNZ_DEV, 3 * NNZ_DEV)
+        passed = pl.ds(2 * NNZ_DEV, NNZ_DEV)
         remote(
-            gathered_blocks[part].at[:, span], gathered_blocks[part].at[:, span],
-            ag_send.at[part], ag_recv.at[part], before(along(part, 1)),
-        ).wait()
-
-    def send_round(r):
-        @pl.loop(0, NPLANE)
+            gathered_blocks[part].at[:, sent], gathered_blocks[part].at[:, sent],
+            ag_send.at[part], pass_recv.at[part], before(along(part, 1)),
+        ).wait_send()
+        remote(
+            gathered_blocks[part].at[:, passed], gathered_blocks[part].at[:, passed],
+            ag_send.at[part], pass_recv.at[part], before(along(part, 1)),
+        ).wait_recv()
+
+    def window(r, part, first, count):
+        if r == 2:
+            base, each = ((0, 4), (128, 8), (384, 4))[part]
+            span = pl.ds(base + each * first, each * count)
+            return s2.at[span], r2.at[span]
+        span = pl.ds(8 * first, 8 * count)
+        if part == 2:
+            return sbufs[r][1].at[span], rbufs[r][1].at[span]
+        rows = pl.ds(part * GROUP, GROUP)
+        return sbufs[r][0].at[span, rows], rbufs[r][0].at[span, rows]
+
+    def send_round(r, late, start, stop):
+        @pl.loop(start, stop)
         def _(i):
             for part in range(3):
                 t = plane_turn(part, i)
                 line = (t, 32 + t, 64 + (t // 8) * 32 + ((t // 2) % 4) * 8 + t % 2)[part]
-                if r == 0:
-                    send, recv, base, count = sbufs[part], rbufs[part], 8 * t, 8
-                    for n in range(8):
-                        block = send_table_s[line, n]
-                        for g in range(2):
-                            send[base + n, g * GROUP:(g + 1) * GROUP] = gathered_blocks[part][g, block]
-                else:
-                    send, recv = s1, r1
-                    base = (4 * t, 128 + 8 * t, 384 + 4 * t)[part]
+                send, recv = window(r, part, t, 1)
+                slots = range(8)
+                if r == 2:
                     slots = ((0, 2, 4, 6), range(8), (1, 3, 5, 7))[part]
-                    count = len(slots)
-                    for n, slot in enumerate(slots):
-                        send[base + n] = gathered_blocks[part][2, send_table_s[line, slot]]
-                span = pl.ds(base, count)
+                for n, slot in enumerate(slots):
+                    send[n] = gathered_blocks[part][r, send_table_s[line, slot]]
 
                 @pl.when(t != 0)
                 def _():
                     remote(
-                        send.at[span], recv.at[span], out_send.at[r, part], out_recv.at[r, part],
+                        send, recv, out_send.at[r, late, part], out_recv.at[r, part],
                         beyond(plane_offset(part, t)),
                     ).start()
 
                 @pl.when(t == 0)
                 def _():
-                    for n in range(count):
-                        recv[base + n] = send[base + n]
-
-    send_round(0)
-    send_round(1)
+                    for n in range(len(slots)):
+                        recv[n] = send[n]
+
+    def issue(r):
+        send_round(r, 0, 0, EARLY)
+        send_round(r, 1, EARLY, NPLANE)
+
+    def wait_sent(r, late):
+        for part in range(3):
+            send, recv = window(r, part, *((EARLY, NPLANE - EARLY) if late else (1, EARLY - 1)))
+            remote(
+                send, recv, out_send.at[r, late, part], out_recv.at[r, part],
+                beyond(along(2, 1)),
+            ).wait_send()
+
+    issue(0)
 
     key_copy.wait()
     own_copy.wait()
@@ -350,17 +393,15 @@
                 ((x + 5 - bx) % 4, (y + 5 - by) % 4, (z + 9 - bz) % 8),
             ).start()
 
-    for r in range(2):
+    for r in range(3):
+        if r < 2:
+            wait_sent(r, 0)
+            issue(r + 1)
         for part in range(3):
-            if r == 0:
-                send, recv, span = sbufs[part], rbufs[part], pl.ds(8, NSLOT - 8)
-            else:
-                send, recv = s1, r1
-                span = (pl.ds(4, 124), pl.ds(136, 248), pl.ds(388, 124))[part]
+            send, recv = window(r, part, 1, NPLANE - 1)
             remote(
-                send.at[span], recv.at[span],
-                out_send.at[r, part], out_recv.at[r, part], beyond(along(2, 1)),
-            ).wait()
+                send, recv, out_send.at[r, 0, part], out_recv.at[r, part], beyond(along(2, 1))
+            ).wait_recv()
 
         high = GROUP * len(ROUND_TOPS[r])
 
@@ -369,16 +410,19 @@
             for b in range(ORB_BLOCKS):
                 p = a * ORB_BLOCKS + b
                 columns = slice(b * BLOCK, (b + 1) * BLOCK)
-                if r == 0:
-                    for part in range(3):
-                        rows = pl.ds(pl.multiple_of(a * high + part * 2 * GROUP, GROUP), 2 * GROUP)
-                        lmat0[rows, columns] = rbufs[part][place_s[part, p]]
+                places = [place_s[part, p] for part in range(3)]
+                if r < 2:
+                    both, third = rbufs[r]
+                    found = (
+                        both[places[0], 0:GROUP], both[places[1], GROUP:2 * GROUP],
+                        third[places[2]],
+                    )
                 else:
-                    rank = place_s[3, p]
-                    one = r1[(place_s[0, p] >> 1) + rank * (384 + (place_s[2, p] >> 1) - (place_s[0, p] >> 1))]
-                    two = r1[128 + place_s[1, p]]
-                    lmat1[pl.ds(pl.multiple_of(a * high, GROUP), GROUP), columns] = one
-                    lmat1[pl.ds(pl.multiple_of(a * high + GROUP, GROUP), GROUP), columns] = two
+                    one, two = places[0] >> 1, 384 + (places[2] >> 1)
+                    found = (r2[one + place_s[3, p] * (two - one)], r2[128 + places[1]])
+                for n, rows in enumerate(found):
+                    top = pl.multiple_of(a * high + n * GROUP, GROUP)
+                    lmats[r][pl.ds(top, GROUP), columns] = rows
 
         def collocate(j):
             cells = pl.ds(pl.multiple_of(j * CHUNK, CHUNK), CHUNK)
@@ -398,13 +442,21 @@
             else:
                 dens[pl.ds(j, 1), :] += line
 
-        if r == 0:
-            pl.loop(0, NCHUNK)(collocate)
+        def collocate_four(j):
+            for n in range(4):
+                collocate(4 * j + n)
+
+        if r < 2:
+            pl.loop(0, NCHUNK // 4)(collocate_four)
         else:
-            pl.loop(0, NCHUNK // 2)(collocate)
+            pl.loop(0, NCHUNK // 8)(collocate_four)
             send_density(0)
-            pl.loop(NCHUNK // 2, NCHUNK)(collocate)
+            pl.loop(NCHUNK // 8, NCHUNK // 4)(collocate_four)
             send_density(1)
+
+    for r in range(3):
+        wait_sent(r, 1)
+    wait_sent(2, 0)
 
     tz[0] = jnp.broadcast_to(jnp.sum(dens[...], keepdims=True), (8, 128))
 
@@ -466,44 +518,49 @@
     mean = total[0:1, 0:1] * (1.0 / TOTAL_CELLS)
     pot_ref[...] = field[1, 8:24, 128:384] - constant_response() * mean
 
-    for q in range(4):
-        send, arrived, per = sbufs[q], rbufs[q], (2, 2, 2, 4)[q]
-        rows_in = [a * BLOCK + q * QUARTER for a in range(ORB_BLOCKS)]
+    def transit(q):
+        if q >= 4:
+            return s2, r2, NSLOT * (q - 4)
+        return ((s0c, r0c), (s0, r0), (s1, r1), (s1c, r1c))[q] + (0,)
+
+    for q, (top, high) in enumerate(PIECES):
+        send, arrived, base = transit(q)
+        depth = ORB_BLOCKS * high
 
         @pl.loop(0, NCHUNK)
         def _(j):
             cells = pl.ds(pl.multiple_of(j * CHUNK, CHUNK), CHUNK)
             line = pot_ref[pl.ds(j, 1), :]
             for a in range(ORB_BLOCKS):
-                scaled[a * QUARTER:(a + 1) * QUARTER, cells] = (
-                    phi_t[rows_in[a]:rows_in[a] + QUARTER, cells].astype(jnp.float32) * line
+                rows = slice(a * BLOCK + top, a * BLOCK + top + high)
+                scaled[a * high:(a + 1) * high, cells] = (
+                    phi_t[rows, cells].astype(jnp.float32) * line
                 ).astype(jnp.bfloat16)
 
-        @pl.loop(0, ORB_BLOCKS // 2)
-        def _(t):
+        def integrate(t):
             columns = pl.ds(pl.multiple_of(t * 2 * BLOCK, 2 * BLOCK), 2 * BLOCK)
             matrix = jnp.dot(
-                scaled[...], phi[:, columns], preferred_element_type=jnp.float32
-            ) * (CELLS ** -0.5)
-            matrix = matrix.astype(jnp.bfloat16)
+                scaled[0:depth], phi[:, columns], preferred_element_type=jnp.float32
+            ).astype(jnp.bfloat16)
             for a in range(ORB_BLOCKS):
                 for j in range(2):
-                    pieces[a * ORB_BLOCKS + 2 * t + j] = matrix[
-                        a * QUARTER:(a + 1) * QUARTER, j * BLOCK:(j + 1) * BLOCK
+                    pieces[a * ORB_BLOCKS + 2 * t + j, 0:high] = matrix[
+                        a * high:(a + 1) * high, j * BLOCK:(j + 1) * BLOCK
                     ]
+
+        if q == 0:
+            for t in range(ORB_BLOCKS // 2):
+                integrate(t)
+        else:
+            pl.loop(0, ORB_BLOCKS // 2)(integrate)
 
         @pl.loop(0, NDEV)
         def _(i):
             offset = turn(i)
             k = number(offset)
             for s in range(2):
-                block = pieces[own_table_s[k, s]]
-                if q < 3:
-                    send[2 * k + s] = block
-                else:
-                    send[4 * k + 2 * s] = block[:GROUP]
-                    send[4 * k + 2 * s + 1] = block[GROUP:]
-            span = pl.ds(per * k, per)
+                send[base + 2 * k + s] = pieces[own_table_s[k, s], 0:high]
+            span = pl.ds(base + 2 * k, 2)
 
             @pl.when(k != 0)
             def _():
@@ -514,33 +571,33 @@
 
             @pl.when(k == 0)
             def _():
-                for n in range(per):
-                    arrived[n] = send[n]
+                for n in range(2):
+                    arrived[base + n] = send[base + n]
 
     order_copy.wait()
-    for q in range(4):
-        send, arrived, per = sbufs[q], rbufs[q], (2, 2, 2, 4)[q]
-        others = pl.ds(per, per * (NDEV - 1))
-        remote(
-            send.at[others], arrived.at[others], back_send.at[q], back_recv.at[q],
-            beyond((0, 0, 0, 1)),
-        ).wait()
+    for group in ((1,), (2,), (0, 3), (4, 5)):
+        for q in group:
+            send, arrived, base = transit(q)
+            others = pl.ds(base + 2, NSLOT - 2)
+            remote(
+                send.at[others], arrived.at[others], back_send.at[q], back_recv.at[q],
+                beyond((0, 0, 0, 1)),
+            ).wait()
 
         def add(n, carry):
             previous, run = carry
             slot, block = order_s[n // 128, n % 128], order_s[2 + n // 128, n % 128]
-            if q < 3:
-                value = arrived[slot].astype(jnp.float32)
-            else:
-                value = jnp.concatenate(
-                    [arrived[2 * slot], arrived[2 * slot + 1]], axis=0
-                ).astype(jnp.float32)
+            held = []
+            for q in group:
+                send, arrived, base = transit(q)
+                held.append(arrived[base + slot].astype(jnp.float32))
+            value = held[0] if len(held) == 1 else jnp.concatenate(held, axis=0)
             run = run * (block == previous).astype(jnp.float32) + value
             sums[n] = run
             return block, run
 
         lax.fori_loop(
-            0, NSLOT, add, (jnp.int32(-1), jnp.zeros((QUARTER, BLOCK), jnp.float32)), unroll=4
+            0, NSLOT, add, (jnp.int32(-1), jnp.zeros((2 * GROUP, BLOCK), jnp.float32)), unroll=4
         )
 
         @pl.loop(0, NNZ_DEV)
@@ -548,7 +605,12 @@
             stop = order_s[4, n]
             start = jnp.where(n == 0, 0, order_s[4, jnp.maximum(n - 1, 0)])
             some = (stop > start).astype(jnp.float32)
-            out_ref[n, q * QUARTER:(q + 1) * QUARTER, :] = sums[jnp.maximum(stop - 1, 0)] * some
+            total = sums[jnp.maximum(stop - 1, 0)] * some
+            into = 0
+            for q in group:
+                top, high = PIECES[q]
+                out_ref[n, top:top + high, :] = total[into:into + high]
+                into += high
 
 
 def body(density_blocks, orbital_values, pair_index):
@@ -557,9 +619,9 @@
     anywhere = pl.BlockSpec(memory_space=pl.ANY)
     dma = pltpu.SemaphoreType.DMA
     bf16, f32, i32 = jnp.bfloat16, jnp.float32, jnp.int32
-    transit = [pltpu.VMEM((NSLOT, 2 * GROUP, BLOCK), bf16)] * 3 + [
-        pltpu.VMEM((2 * NSLOT, GROUP, BLOCK), bf16)
-    ]
+    transit = [
+        pltpu.VMEM((NSLOT, 2 * GROUP, BLOCK), bf16), pltpu.VMEM((NSLOT, GROUP, BLOCK), bf16)
+    ] * 2 + [pltpu.VMEM((2 * NSLOT, GROUP, BLOCK), bf16)]
     summed, pot = pl.pallas_call(
         main_kernel,
         out_shape=(
@@ -576,9 +638,9 @@
         ] + transit + transit + [
             pltpu.VMEM((ORB_BLOCKS * GROUP * len(tops), LOCAL_ORB), bf16) for tops in ROUND_TOPS
         ] + [
-            pltpu.VMEM((ORB_BLOCKS * QUARTER, CELLS), bf16),
-            pltpu.VMEM((NPAIR, QUARTER, BLOCK), bf16),
-            pltpu.VMEM((NSLOT, QUARTER, BLOCK), f32),
+            pltpu.VMEM((2 * GROUP * ORB_BLOCKS, CELLS), bf16),
+            pltpu.VMEM((NPAIR, 2 * GROUP, BLOCK), bf16),
+            pltpu.VMEM((NSLOT, 2 * GROUP, BLOCK), f32),
             pltpu.VMEM((NDEV, 1, 128), i32),
             pltpu.VMEM((NDEV, 128), i32),
             pltpu.VMEM((1, 128), i32),
@@ -599,8 +661,8 @@
             pltpu.VMEM((8, 8, 128), f32),
             pltpu.VMEM((4, 8, 128), f32),
             pltpu.VMEM((4, 8, 128), f32),
-            dma, dma((4,)), dma((3,)), dma((3,)), dma((3,)), dma((3,)), dma((2, 3)), dma((2, 3)),
-            dma((2,)), dma((2,)), dma((3,)), dma((3,)), dma((4,)), dma((4,)),
+            dma, dma((4,)), dma((3,)), dma((3,)), dma((3,)), dma((3, 3, 2)), dma((3,)), dma((3, 2, 3)), dma((3, 3)),
+            dma((2,)), dma((2,)), dma((3,)), dma((3,)), dma((6,)), dma((6,)),
         ],
         compiler_params=pltpu.CompilerParams(
             collective_id=0, has_side_effects=True, vmem_limit_bytes=61 * 2**20
@@ -610,7 +672,7 @@
         ),
         name="collocate_solve_integrate",
     )(pair_index, density_blocks, phi)
-    return summed, pot.reshape(16, 16, 16)
+    return summed * CELLS ** -0.5, pot.reshape(16, 16, 16)
 
 
 def solution(mesh):

time: 229 us -> 217 us (0.948)
  Pallas kernels: 223 us -> 212 us
  local copies, waits for them, and re-layouts: 4.6 us -> 0.76 us
  other arithmetic: 0 us -> 3.15 us
    pallas_call x1, Pallas kernels: 223 us -> 212 us  [body(): pl.pallas_call(main_kernel, out_shape=(jax.ShapeDtypeStruct((NNZ_DEV, BLO...]
    mul x0 -> x1, other arithmetic: none -> 3.15 us  [body(): return (summed * CELLS ** (-0.5), pot.reshape(16, 16, 16))]
    unnamed x1 -> x2, local copies, waits for them, and re-layouts: 3.13 us -> 0.01 us
where the time goes in v4:
time: 217 us
  Pallas kernels  212 us (98%)
  other arithmetic  3.15 us (1%)
    pallas_call x1, Pallas kernels, body(): pl.pallas_call(main_kernel, out_shape=(jax.ShapeDtypeStruct((NNZ_DEV, BLO...  212 us

profile of v4, /device:TPU:0, one launch (start us, length us, event | category | flops | bytes accessed | tf_op | source)
XLA Modules:
  0.0 216.6 jit_solution(3999444772019445209)
XLA Ops:
  0.6 212.1 %collocate_solve_integrate.1 = (f32[32,128,128]{2,1,0:T(8,128)}, f32[16,256]{1,0:T(8,128)}) custom-call(s32[1,100]{1,0:T(1,128)} %own_ref.1, bf16[32,128,128]{2,1,0:T(8,128)(2,1)} %blocks_ref.1, bf16[4096,1280]{1,0:T(8,128)(2,1)} %bitcast.1), custom_call_target="tpu_custom_call" | custom-call | flops 26843545600 | bytes 41943040 | tf_op jit(solution)/shard_map/collocate_solve_integrate/pallas_call | solution.py:625
  212.7 0.0 copy-start
  212.7 3.1 %broadcast_multiply_fusion = f32[32,128,128]{2,1,0:T(8,128)} fusion(f32[32,128,128]{2,1,0:T(8,128)} %get-tuple-element.4), kind=kLoop, calls=%fused_computation | loop fusion | flops 524288 | bytes 4194304 | tf_op jit(solution)/shard_map/mul | solution.py:675
  215.9 0.0 copy-done
  215.9 0.8 reshape.11
Async XLA Ops:
  212.7 3.2 %copy-start = (f32[16,256]{1,0:T(8,128)S(1)}, f32[16,256]{1,0:T(8,128)}, u32[]{:S(2)}) copy-start(f32[16,256]{1,0:T(8,128)} %get-tuple-element.5) | copy-start | bytes 49156

commit v5 on v4

--- a/solution.py
+++ b/solution.py
@@ -21,10 +21,10 @@
 NCHUNK = CELLS // CHUNK
 TOTAL_CELLS = 524288
 GROUP = 16
-PIECES = ((0, 16), (16, 32), (48, 32), (80, 16), (96, 16), (112, 16))
 EARLY = 26
 PARTS = ((0, 16, 32), (48, 64, 80), (96, 112, 32))
 ROUND_TOPS = ((0, 48, 96), (16, 64, 112), (32, 80))
+DIRECT = (32, 80)
 
 
 OMEGA = 0.6
@@ -148,11 +148,12 @@
     s0, s0c, s1, s1c, s2,
     r0, r0c, r1, r1c, r2,
     lmat0, lmat1, lmat2, scaled, pieces, sums,
-    asked, own_table, own_key, send_table, order,
+    asked, asked_c, own_table, own_key, send_table, order,
     own_table_s, own_key_s, send_table_s, place_s, order_s,
     dens, near, source, pre, field, coarse, corr, tz, ty, tx,
     phi_sem, local_sem, ask_send, ask_recv, ag_send, ag_recv, pass_recv, out_send, out_recv,
     near_send, near_recv, tot_send, tot_recv, back_send, back_recv,
+    relay_send, relay_recv, sum_send, sum_recv,
 ):
     gathered_blocks = (ag_a, ag_b, ag_c)
     sbufs, rbufs = ((s0, s0c), (s1, s1c), (s2,)), ((r0, r0c), (r1, r1c), (r2,))
@@ -246,6 +247,14 @@
         jnp.concatenate([wanted[n * 32:n * 32 + 8] for n in range(4)], axis=0),
         wanted,
     )
+
+    def holder_at(axis, j):
+        return (
+            ((x + j) % 4) * 32 + y * 8 + w * 2 + c,
+            x * 32 + ((y + j) % 4) * 8 + w * 2 + c,
+            x * 32 + y * 8 + ((w + j) % 4) * 2 + c,
+        )[axis]
+
     for axis, base in enumerate((0, 32, 64)):
         ask = asks[axis]
         count = ask.shape[0]
@@ -253,11 +262,7 @@
         value = lane_n * 32 + (ask & 31)
         table = jnp.zeros((count, 128), jnp.int32)
         for j in range(4):
-            holder = (
-                ((x + j) % 4) * 32 + y * 8 + w * 2 + c,
-                x * 32 + ((y + j) % 4) * 8 + w * 2 + c,
-                x * 32 + y * 8 + ((w + j) % 4) * 2 + c,
-            )[axis]
+            holder = holder_at(axis, j)
             first, last = first_last(
                 ((ask >> 5) == holder) & (lane_n < NPAIR), value, 0, NNZ_DEV * 128 - 1
             )
@@ -342,31 +347,50 @@
         place_s[2, p] = (dx * 8 + dy * 2 + (k & 1)) * 8 + ((4 - dw) & 3) * 2 + rank
         place_s[3, p] = rank
 
+    def sort_slots(base, firsts, lasts, above, slots, none):
+        blocks = [
+            jnp.where(lasts >= 0, above + (firsts & 31), none),
+            jnp.where(lasts > firsts, above + (lasts & 31), none),
+        ]
+        keys = [block * NSLOT + slot for block, slot in zip(blocks, slots)]
+        across = [jnp.broadcast_to(key, (NDEV, 128)).T for key in keys]
+        ranks = [
+            sum(jnp.sum((other < key).astype(jnp.int32), axis=1, keepdims=True) for other in across)
+            for key in keys
+        ]
+        for n in range(2):
+            at = [rank == lane + 128 * n for rank in ranks]
+            order[base + n:base + n + 1] = sum(
+                jnp.sum(jnp.where(a, slot, 0), axis=0, keepdims=True) for a, slot in zip(at, slots)
+            )
+            order[base + 2 + n:base + 3 + n] = sum(
+                jnp.sum(jnp.where(a, block, 0), axis=0, keepdims=True)
+                for a, block in zip(at, blocks)
+            )
+        order[base + 4:base + 5] = sum(
+            jnp.sum((block <= lane).astype(jnp.int32), axis=0, keepdims=True) for block in blocks
+        )
+        order[base + 5:base + 8] = jnp.zeros((3, 128), jnp.int32)
+
+    count = row[:, 0:1]
     first, last = first_last(
         ((wanted >> 5) == me) & (lane < NPAIR), lane * 32 + (wanted & 31), -1, NNZ_DEV * 128
     )
-    blocks = [
-        jnp.where(last >= 0, first & 31, NNZ_DEV), jnp.where(last > first, last & 31, NNZ_DEV)
-    ]
-    slots = [2 * row[:, 0:1], 2 * row[:, 0:1] + 1]
-    keys = [block * NSLOT + slot for block, slot in zip(blocks, slots)]
-    across = [jnp.broadcast_to(key, (NDEV, 128)).T for key in keys]
-    ranks = [
-        sum(jnp.sum((other < key).astype(jnp.int32), axis=1, keepdims=True) for other in across)
-        for key in keys
-    ]
-    for n in range(2):
-        at = [rank == lane + 128 * n for rank in ranks]
-        order[n:n + 1] = sum(
-            jnp.sum(jnp.where(a, slot, 0), axis=0, keepdims=True) for a, slot in zip(at, slots)
-        )
-        order[2 + n:3 + n] = sum(
-            jnp.sum(jnp.where(a, block, 0), axis=0, keepdims=True) for a, block in zip(at, blocks)
-        )
-    order[4:5] = sum(
-        jnp.sum((block <= lane).astype(jnp.int32), axis=0, keepdims=True) for block in blocks
-    )
-    order[5:8] = jnp.zeros((3, 128), jnp.int32)
+    sort_slots(0, first, last, 0, (2 * count, 2 * count + 1), NNZ_DEV)
+    for n in range(16):
+        asked_c[2 * n:2 * n + 2] = asked[8 * n:8 * n + 2, 0, :]
+    for part in range(3):
+        ask = asks[part] if part < 2 else asked_c[...]
+        pairs = [
+            first_last(
+                ((ask >> 5) == holder_at(part, j)) & (lane[0:NPLANE] < NPAIR),
+                lane[0:NPLANE] * 32 + (ask & 31), -1, NNZ_DEV * 128,
+            )
+            for j in range(4)
+        ]
+        first, last = (jnp.concatenate(side, axis=0) for side in zip(*pairs))
+        slot = (count & 31) * 8 + (count >> 5) * 2
+        sort_slots(8 + 8 * part, first, last, count & 96, (slot, slot + 1), NDEV)
     order_copy = pltpu.make_async_copy(order, order_s, local_sem.at[3])
     order_copy.start()
 
@@ -518,13 +542,8 @@
     mean = total[0:1, 0:1] * (1.0 / TOTAL_CELLS)
     pot_ref[...] = field[1, 8:24, 128:384] - constant_response() * mean
 
-    def transit(q):
-        if q >= 4:
-            return s2, r2, NSLOT * (q - 4)
-        return ((s0c, r0c), (s0, r0), (s1, r1), (s1c, r1c))[q] + (0,)
-
-    for q, (top, high) in enumerate(PIECES):
-        send, arrived, base = transit(q)
+    def integrate(tops, unroll):
+        high = GROUP * len(tops)
         depth = ORB_BLOCKS * high
 
         @pl.loop(0, NCHUNK)
@@ -532,12 +551,13 @@
             cells = pl.ds(pl.multiple_of(j * CHUNK, CHUNK), CHUNK)
             line = pot_ref[pl.ds(j, 1), :]
             for a in range(ORB_BLOCKS):
-                rows = slice(a * BLOCK + top, a * BLOCK + top + high)
-                scaled[a * high:(a + 1) * high, cells] = (
-                    phi_t[rows, cells].astype(jnp.float32) * line
-                ).astype(jnp.bfloat16)
-
-        def integrate(t):
+                for n, top in enumerate(tops):
+                    rows = slice(a * BLOCK + top, a * BLOCK + top + GROUP)
+                    scaled[a * high + n * GROUP:a * high + (n + 1) * GROUP, cells] = (
+                        phi_t[rows, cells].astype(jnp.float32) * line
+                    ).astype(jnp.bfloat16)
+
+        def multiply(t):
             columns = pl.ds(pl.multiple_of(t * 2 * BLOCK, 2 * BLOCK), 2 * BLOCK)
             matrix = jnp.dot(
                 scaled[0:depth], phi[:, columns], preferred_element_type=jnp.float32
@@ -548,69 +568,165 @@
                         a * high:(a + 1) * high, j * BLOCK:(j + 1) * BLOCK
                     ]
 
-        if q == 0:
+        if unroll:
             for t in range(ORB_BLOCKS // 2):
-                integrate(t)
+                multiply(t)
         else:
-            pl.loop(0, ORB_BLOCKS // 2)(integrate)
+            pl.loop(0, ORB_BLOCKS // 2)(multiply)
+
+    def send_direct(q):
+        base = NSLOT * q
 
         @pl.loop(0, NDEV)
         def _(i):
             offset = turn(i)
             k = number(offset)
             for s in range(2):
-                send[base + 2 * k + s] = pieces[own_table_s[k, s], 0:high]
+                s2[base + 2 * k + s] = pieces[own_table_s[k, s], 0:GROUP]
             span = pl.ds(base + 2 * k, 2)
 
             @pl.when(k != 0)
             def _():
                 remote(
-                    send.at[span], arrived.at[span], back_send.at[q], back_recv.at[q],
-                    before(offset),
+                    s2.at[span], r2.at[span], back_send.at[q], back_recv.at[q], before(offset)
                 ).start()
 
             @pl.when(k == 0)
             def _():
                 for n in range(2):
-                    arrived[base + n] = send[base + n]
-
+                    r2[base + n] = s2[base + n]
+
+    def send_relays(r):
+        @pl.loop(0, NPLANE)
+        def _(i):
+            for part in range(3):
+                t = plane_turn(part, i)
+                send, recv = window(r, part, t, 1)
+                for n in range(8):
+                    offset = list(plane_offset(part, t))
+                    offset[part] = (4 - n // 2) % 4
+                    send[n] = pieces[
+                        own_table_s[number(offset), n % 2], part * GROUP:(part + 1) * GROUP
+                    ]
+
+                @pl.when(t != 0)
+                def _():
+                    remote(
+                        send, recv, relay_send.at[r, part], relay_recv.at[r, part],
+                        before(plane_offset(part, t)),
+                    ).start()
+
+                @pl.when(t == 0)
+                def _():
+                    for n in range(8):
+                        recv[n] = send[n]
+
+    def segment_sums(takes):
+        def add(n, carry):
+            following = []
+            for g, ((base, take), (previous, run)) in enumerate(zip(takes, carry)):
+                slot = order_s[base + n // 128, n % 128]
+                block = order_s[base + 2 + n // 128, n % 128]
+                run = run * (block == previous).astype(jnp.float32) + take(slot).astype(jnp.float32)
+                sums[n, g * GROUP:(g + 1) * GROUP] = run
+                following.append((block, run))
+            return tuple(following)
+
+        empty = (jnp.int32(-1), jnp.zeros((GROUP, BLOCK), jnp.float32))
+        lax.fori_loop(0, NSLOT, add, (empty,) * len(takes), unroll=4)
+
+    def segment(base, g, n):
+        stop = order_s[base + 4, n]
+        start = jnp.where(n == 0, 0, order_s[base + 4, jnp.maximum(n - 1, 0)])
+        some = (stop > start).astype(jnp.float32)
+        return sums[jnp.maximum(stop - 1, 0), g * GROUP:(g + 1) * GROUP] * some
+
+    def relay(r):
+        for part in range(3):
+            send, recv = window(r, part, 1, NPLANE - 1)
+            remote(
+                send, recv, relay_send.at[r, part], relay_recv.at[r, part], beyond(along(2, 1))
+            ).wait_recv()
+        for parts in ((0, 1), (2,)):
+            takes = []
+            for part in parts:
+                if part < 2:
+                    takes.append((8 + 8 * part, lambda slot, part=part: rbufs[r][0][
+                        slot, part * GROUP:(part + 1) * GROUP]))
+                else:
+                    takes.append((8 + 8 * part, lambda slot: rbufs[r][1][slot]))
+            segment_sums(takes)
+            for g, part in enumerate(parts):
+                held = gathered_blocks[part]
+                if r == 1:
+                    sum_copy(0, part).wait_send()
+
+                @pl.loop(0, NNZ_DEV)
+                def _(n):
+                    held[r, n] = segment(8 + 8 * part, g, n).astype(jnp.bfloat16)
+
+                @pl.loop(NNZ_DEV, 4 * NNZ_DEV)
+                def _(n):
+                    held[2, n] = segment(8 + 8 * part, g, n).astype(jnp.bfloat16)
+
+                for j in (1, 3, 2):
+                    span = pl.ds(j * NNZ_DEV, NNZ_DEV)
+                    remote(
+                        held.at[2, span], held.at[r, span],
+                        sum_send.at[r, part], sum_recv.at[r, part], beyond(along(part, j)),
+                    ).start()
+
+    def sum_copy(r, part):
+        span = pl.ds(NNZ_DEV, 3 * NNZ_DEV)
+        return remote(
+            gathered_blocks[part].at[2, span], gathered_blocks[part].at[r, span],
+            sum_send.at[r, part], sum_recv.at[r, part], beyond(along(part, 1)),
+        )
+
+    def finish(r):
+        for part in range(3):
+            sum_copy(r, part).wait_recv()
+            held, top = gathered_blocks[part], PARTS[part][r]
+
+            @pl.loop(0, NNZ_DEV // 4)
+            def _(m):
+                for u in range(4):
+                    n = 4 * m + u
+                    out_ref[n, top:top + GROUP, :] = sum(
+                        held[r, j * NNZ_DEV + n].astype(jnp.float32) for j in range(4)
+                    )
+
+    integrate(DIRECT[0:1], True)
+    send_direct(0)
+    for r in range(2):
+        integrate(ROUND_TOPS[r], False)
+        send_relays(r)
     order_copy.wait()
-    for group in ((1,), (2,), (0, 3), (4, 5)):
-        for q in group:
-            send, arrived, base = transit(q)
-            others = pl.ds(base + 2, NSLOT - 2)
+    relay(0)
+    integrate(DIRECT[1:2], True)
+    send_direct(1)
+    relay(1)
+    finish(0)
+    for q in range(2):
+        others = pl.ds(NSLOT * q + 2, NSLOT - 2)
+        remote(
+            s2.at[others], r2.at[others], back_send.at[q], back_recv.at[q], beyond(along(2, 1))
+        ).wait()
+    segment_sums([(0, lambda slot: r2[slot]), (0, lambda slot: r2[NSLOT + slot])])
+
+    @pl.loop(0, NNZ_DEV)
+    def _(n):
+        for g, top in enumerate(DIRECT):
+            out_ref[n, top:top + GROUP, :] = segment(0, g, n)
+
+    finish(1)
+    for part in range(3):
+        sum_copy(1, part).wait_send()
+        for r in range(2):
+            send, recv = window(r, part, 1, NPLANE - 1)
             remote(
-                send.at[others], arrived.at[others], back_send.at[q], back_recv.at[q],
-                beyond((0, 0, 0, 1)),
-            ).wait()
-
-        def add(n, carry):
-            previous, run = carry
-            slot, block = order_s[n // 128, n % 128], order_s[2 + n // 128, n % 128]
-            held = []
-            for q in group:
-                send, arrived, base = transit(q)
-                held.append(arrived[base + slot].astype(jnp.float32))
-            value = held[0] if len(held) == 1 else jnp.concatenate(held, axis=0)
-            run = run * (block == previous).astype(jnp.float32) + value
-            sums[n] = run
-            return block, run
-
-        lax.fori_loop(
-            0, NSLOT, add, (jnp.int32(-1), jnp.zeros((2 * GROUP, BLOCK), jnp.float32)), unroll=4
-        )
-
-        @pl.loop(0, NNZ_DEV)
-        def _(n):
-            stop = order_s[4, n]
-            start = jnp.where(n == 0, 0, order_s[4, jnp.maximum(n - 1, 0)])
-            some = (stop > start).astype(jnp.float32)
-            total = sums[jnp.maximum(stop - 1, 0)] * some
-            into = 0
-            for q in group:
-                top, high = PIECES[q]
-                out_ref[n, top:top + high, :] = total[into:into + high]
-                into += high
+                send, recv, relay_send.at[r, part], relay_recv.at[r, part], beyond(along(2, 1))
+            ).wait_send()
 
 
 def body(density_blocks, orbital_values, pair_index):
@@ -638,19 +754,20 @@
         ] + transit + transit + [
             pltpu.VMEM((ORB_BLOCKS * GROUP * len(tops), LOCAL_ORB), bf16) for tops in ROUND_TOPS
         ] + [
-            pltpu.VMEM((2 * GROUP * ORB_BLOCKS, CELLS), bf16),
-            pltpu.VMEM((NPAIR, 2 * GROUP, BLOCK), bf16),
+            pltpu.VMEM((3 * GROUP * ORB_BLOCKS, CELLS), bf16),
+            pltpu.VMEM((NPAIR, 3 * GROUP, BLOCK), bf16),
             pltpu.VMEM((NSLOT, 2 * GROUP, BLOCK), f32),
             pltpu.VMEM((NDEV, 1, 128), i32),
+            pltpu.VMEM((NPLANE, 128), i32),
             pltpu.VMEM((NDEV, 128), i32),
             pltpu.VMEM((1, 128), i32),
             pltpu.VMEM((192, 128), i32),
-            pltpu.VMEM((8, 128), i32),
+            pltpu.VMEM((32, 128), i32),
             pltpu.SMEM((NDEV, 128), i32),
             pltpu.SMEM((1, 128), i32),
             pltpu.SMEM((192, 128), i32),
             pltpu.SMEM((4, 128), i32),
-            pltpu.SMEM((8, 128), i32),
+            pltpu.SMEM((32, 128), i32),
             pltpu.VMEM((16, 256), f32),
             pltpu.VMEM((2, 26, 8, 256), f32),
             pltpu.VMEM((3, 48, 768), f32),
@@ -662,10 +779,11 @@
             pltpu.VMEM((4, 8, 128), f32),
             pltpu.VMEM((4, 8, 128), f32),
             dma, dma((4,)), dma((3,)), dma((3,)), dma((3,)), dma((3, 3, 2)), dma((3,)), dma((3, 2, 3)), dma((3, 3)),
-            dma((2,)), dma((2,)), dma((3,)), dma((3,)), dma((6,)), dma((6,)),
+            dma((2,)), dma((2,)), dma((3,)), dma((3,)), dma((2,)), dma((2,)),
+            dma((2, 3)), dma((2, 3)), dma((2, 3)), dma((2, 3)),
         ],
         compiler_params=pltpu.CompilerParams(
-            collective_id=0, has_side_effects=True, vmem_limit_bytes=61 * 2**20
+            collective_id=0, has_side_effects=True, vmem_limit_bytes=62 * 2**20
         ),
         cost_estimate=pl.CostEstimate(
             flops=4 * CELLS * LOCAL_ORB * LOCAL_ORB, bytes_accessed=40 * 2**20, transcendentals=0

time: 217 us -> 206 us (0.949)
  Pallas kernels: 212 us -> 201 us
    pallas_call x1, Pallas kernels: 212 us -> 201 us  [body(): pl.pallas_call(main_kernel, out_shape=(jax.ShapeDtypeStruct((NNZ_DEV, BLO...]
where the time goes in v5:
time: 206 us; the launch traced here: 205 us
  Pallas kernels  201 us (98%)
  other arithmetic  3.15 us (2%)
    pallas_call x1, Pallas kernels, body(): pl.pallas_call(main_kernel, out_shape=(jax.ShapeDtypeStruct((NNZ_DEV, BLO...  201 us

profile of v5, /device:TPU:0, one launch (start us, length us, event | category | flops | bytes accessed | tf_op | source)
XLA Modules:
  0.0 205.5 jit_solution(3484904966182757395)
XLA Ops:
  0.6 200.9 %collocate_solve_integrate.1 = (f32[32,128,128]{2,1,0:T(8,128)}, f32[16,256]{1,0:T(8,128)}) custom-call(s32[1,100]{1,0:T(1,128)} %own_ref.1, bf16[32,128,128]{2,1,0:T(8,128)(2,1)} %blocks_ref.1, bf16[4096,1280]{1,0:T(8,128)(2,1)} %bitcast.1), custom_call_target="tpu_custom_call" | custom-call | flops 26843545600 | bytes 41943040 | tf_op jit(solution)/shard_map/collocate_solve_integrate/pallas_call | solution.py:741
  201.5 0.0 copy-start
  201.5 3.1 %broadcast_multiply_fusion = f32[32,128,128]{2,1,0:T(8,128)} fusion(f32[32,128,128]{2,1,0:T(8,128)} %get-tuple-element.4), kind=kLoop, calls=%fused_computation | loop fusion | flops 524288 | bytes 4194304 | tf_op jit(solution)/shard_map/mul | solution.py:793
  204.7 0.0 copy-done
  204.7 0.8 reshape.11
Async XLA Ops:
  201.5 3.2 %copy-start = (f32[16,256]{1,0:T(8,128)S(1)}, f32[16,256]{1,0:T(8,128)}, u32[]{:S(2)}) copy-start(f32[16,256]{1,0:T(8,128)} %get-tuple-element.5) | copy-start | bytes 49156

commit v6 on v5

--- a/solution.py
+++ b/solution.py
@@ -21,7 +21,7 @@
 NCHUNK = CELLS // CHUNK
 TOTAL_CELLS = 524288
 GROUP = 16
-EARLY = 26
+EARLY = 16
 PARTS = ((0, 16, 32), (48, 64, 80), (96, 112, 32))
 ROUND_TOPS = ((0, 48, 96), (16, 64, 112), (32, 80))
 DIRECT = (32, 80)
@@ -702,8 +702,8 @@
         integrate(ROUND_TOPS[r], False)
         send_relays(r)
     order_copy.wait()
+    integrate(DIRECT[1:2], True)
     relay(0)
-    integrate(DIRECT[1:2], True)
     send_direct(1)
     relay(1)
     finish(0)

time: 206 us -> 206 us (level)
  no operation moved by 1% of the time
where the time goes in v6:
time: 206 us; the launch traced here: 205 us
  Pallas kernels  201 us (98%)
  other arithmetic  3.15 us (2%)
    pallas_call x1, Pallas kernels, body(): pl.pallas_call(main_kernel, out_shape=(jax.ShapeDtypeStruct((NNZ_DEV, BLO...  201 us

profile of v6, /device:TPU:0, one launch (start us, length us, event | category | flops | bytes accessed | tf_op | source)
XLA Modules:
  0.0 205.3 jit_solution(857222503664643112)
XLA Ops:
  0.6 200.8 %collocate_solve_integrate.1 = (f32[32,128,128]{2,1,0:T(8,128)}, f32[16,256]{1,0:T(8,128)}) custom-call(s32[1,100]{1,0:T(1,128)} %own_ref.1, bf16[32,128,128]{2,1,0:T(8,128)(2,1)} %blocks_ref.1, bf16[4096,1280]{1,0:T(8,128)(2,1)} %bitcast.1), custom_call_target="tpu_custom_call" | custom-call | flops 26843545600 | bytes 41943040 | tf_op jit(solution)/shard_map/collocate_solve_integrate/pallas_call | solution.py:741
  201.4 0.0 copy-start
  201.4 3.1 %broadcast_multiply_fusion = f32[32,128,128]{2,1,0:T(8,128)} fusion(f32[32,128,128]{2,1,0:T(8,128)} %get-tuple-element.4), kind=kLoop, calls=%fused_computation | loop fusion | flops 524288 | bytes 4194304 | tf_op jit(solution)/shard_map/mul | solution.py:793
  204.6 0.0 copy-done
  204.6 0.8 reshape.11
Async XLA Ops:
  201.4 3.2 %copy-start = (f32[16,256]{1,0:T(8,128)S(1)}, f32[16,256]{1,0:T(8,128)}, u32[]{:S(2)}) copy-start(f32[16,256]{1,0:T(8,128)} %get-tuple-element.5) | copy-start | bytes 49156
